TPU v7x, 768 devices: a whole 4x8x12 slice. The times are simulated.
768 devices in a mesh: blk: 16 (over z_hi, y), pairs: 48 (over z_lo, x, core).
Axes of the slice: x: 4, y: 8, z: 12 (z_hi: 2, z_lo: 6; z = z_hi * 6 + z_lo), core: 2. Of those that a mesh axis runs over, the one named last changes fastest.
Arguments:
- amplitudes: bfloat16 [3072, 48, 4096], P(('blk', 'pairs')), may hold values from -6 to 6
- integrals: bfloat16 [1024, 48, 4096], P('blk', 'pairs'), may hold values from -0.013671875 to 0.013671875
- amp_pattern: int32 [16, 256], replicated, may hold values 0 or 1
- int_pattern: int32 [16, 256], replicated, may hold values 0 or 1
- slab_ids: int32 [48], replicated, may hold values from 0 to 255, as said below
- pair_window: int32 [2, 3072], replicated, may hold values from 0 to 199
Outputs:
- ladder: float32 [3072, 1024], P(('blk', 'pairs'))
Inputs may be any that keep to these rules, and one draw needn't show every extreme that they name: `slab_ids`: the entries are distinct; 0 and 255 are always among them.
All inputs are finite; a program needn't handle non-finite values.
Results may differ from a plain program's by a relative error of at most 0.0003.
Values may be sent and summed in bfloat16 or wider, within the bound.
No kernel may reach another device: no remote copies, remote signals or barrier semaphores. Data moves between devices by JAX's collectives and lax.ppermute only.
A program may use at most 64 MiB of HBM per device.

v0:
```python
import jax
import jax.numpy as jnp
from jax import lax
from jax.sharding import PartitionSpec as P

TILE = 64
NOCC = 200


def table_rows(index_list, width):
    return (index_list[:, None] == jnp.arange(width, dtype=jnp.int32)[None, :]).astype(jnp.float32)


def lookup(row_ids, pattern, slab_local):
    occ_onehot = table_rows(row_ids, pattern.shape[0])
    slab_onehot = table_rows(slab_local, pattern.shape[1])
    picked = jnp.dot(occ_onehot, pattern.astype(jnp.float32), precision=lax.Precision.HIGHEST)
    return jnp.dot(picked, slab_onehot.T, precision=lax.Precision.HIGHEST)


def per_device(amplitudes, integrals, amp_pattern, int_pattern, slab_ids, pair_window):
    block_index = lax.axis_index("blk")
    owner_index = lax.axis_index("pairs")
    block_count = lax.axis_size("blk")
    regrouped = lax.all_to_all(amplitudes, "pairs", split_axis=1, concat_axis=0, tiled=True)
    group_pairs = regrouped.shape[0]
    slab_local = regrouped.shape[1]
    occ_tiles = (NOCC + TILE - 1) // TILE
    my_slab = lax.dynamic_slice_in_dim(slab_ids, owner_index * slab_local, slab_local)
    my_window = lax.dynamic_slice_in_dim(pair_window, block_index * group_pairs, group_pairs, 1)
    occ_tile = my_window[0] // TILE * occ_tiles + my_window[1] // TILE
    amp_mask = lookup(occ_tile, amp_pattern, my_slab)
    masked_amp = regrouped * amp_mask[:, :, None].astype(jnp.bfloat16)
    block_rows = integrals.shape[0]
    row_total = block_rows * block_count
    row_tiles = jnp.arange(row_total, dtype=jnp.int32) // TILE
    int_mask = lookup(row_tiles, int_pattern, my_slab)
    contract = (((1, 2), (1, 2)), ((), ()))
    weights = lax.all_gather(integrals, "blk", axis=0, tiled=True) * int_mask[:, :, None].astype(
        jnp.bfloat16
    )
    product = lax.dot_general(masked_amp, weights, contract, preferred_element_type=jnp.float32)
    return lax.psum_scatter(product, "pairs", scatter_dimension=0, tiled=True)


def solution(mesh):
    placed = (P(("blk", "pairs"), None, None), P("blk", "pairs", None), P(), P(), P(), P())
    return jax.shard_map(
        per_device, mesh=mesh, in_specs=placed, out_specs=P(("blk", "pairs"), None), check_vma=False
    )
```

profile of v0, /device:TPU:1, one launch (start us, length us, event | category | flops | bytes accessed | tf_op | source)
XLA Modules:
  0.0 859.2 jit_solution(4623587817327722014)
XLA Ops:
  6.5 0.0 all-gather.2.cloned.1.call-start
  6.5 0.7 all-gather.2.cloned.1.call-update
  7.3 3.8 copy.9
  11.1 0.0 copy-start.2
  11.1 0.0 copy-start.1
  11.1 0.0 copy-start
  11.1 16.6 %all-to-all-start = ((bf16[4,48,4096]{2,0,1:T(4,128)(2,1)}), bf16[4,48,4096]{2,0,1:T(4,128)(2,1)S(1)}, u32[]{:S(2)}, u32[]{:S(2)}) async-start(bf16[4,48,4096]{2,0,1:T(4,128)(2,1)} %copy.9), calls=%async_computation | async-start | bytes 3145728 | tf_op jit(solution)/shard_map/all_to_all | solution.py:25
  27.6 0.0 all-reduce.3.cloned.1.call-start
  27.7 0.0 copy-done.2
  27.7 0.6 dynamic_slice.7
  28.3 0.6 iota_compare_fusion.4
  29.0 0.8 constant_dynamic-slice_fusion.1
  29.8 0.0 copy-done.1
  29.8 0.3 fusion.6
  30.1 0.2 fusion.14
  30.3 0.2 mul.40
  30.5 0.0 copy-done
  30.5 0.6 fusion.4
  31.1 0.6 fusion.15
  31.7 69.3 %all-to-all-done = bf16[4,48,4096]{2,0,1:T(4,128)(2,1)S(1)} async-done(((bf16[4,48,4096]{2,0,1:T(4,128)(2,1)}), bf16[4,48,4096]{2,0,1:T(4,128)(2,1)S(1)}, u32[]{:S(2)}, u32[]{:S(2)}) %all-to-all-start) | async-done | bytes 1572896 | tf_op jit(solution)/shard_map/all_to_all | solution.py:25
  101.0 0.8 bitcast_multiply_fusion
  101.8 0.4 mul.43
  102.2 170.3 %all-gather.2.cloned.1.call-done = bf16[1024,1,4096]{2,0,1:T(8,128)(2,1)} async-done(((bf16[64,1,4096]{2,0,1:T(8,128)(2,1)}), bf16[1024,1,4096]{2,0,1:T(8,128)(2,1)}) %all-gather.2.cloned.1.call-update) | async-done | bytes 8388624 | tf_op jit(solution)/shard_map/all_gather | solution.py:39
  272.5 7.3 fusion
  279.8 0.0 all-reduce.3.cloned.1.call-update
  279.8 1.3 dynamic-slice
  281.8 569.3 %all-reduce.3.cloned.1.call-done = f32[192,1024]{1,0:T(8,128)} async-done(((f32[192,1024]{1,0:T(8,128)}), f32[192,1024]{1,0:T(8,128)}) %all-reduce.3.cloned.1.call-update) | async-done | bytes 786448
  851.0 1.4 constant_dynamic-slice_fusion
  (5 shorter events, 0.0 us)
Async XLA Ops:
  6.5 266.0 %all-gather.2.cloned.1.call-start = ((), (), s32[]{:S(2)}) async-start(), calls=%async_computation.1 | async-start | bytes 8912896 | tf_op jit(solution)/shard_map/all_gather | solution.py:39
  11.1 16.6 %copy-start.2 = (s32[48]{0:T(128)S(1)}, s32[48]{0:T(128)}, u32[]{:S(2)}) copy-start(s32[48]{0:T(128)} %param.10) | copy-start | bytes 580
  11.1 18.8 %copy-start.1 = (s32[16,256]{1,0:T(8,128)S(1)}, s32[16,256]{1,0:T(8,128)}, u32[]{:S(2)}) copy-start(s32[16,256]{1,0:T(8,128)} %param.8) | copy-start | bytes 49156
  11.1 19.4 %copy-start = (s32[16,256]{1,0:T(8,128)S(1)}, s32[16,256]{1,0:T(8,128)}, u32[]{:S(2)}) copy-start(s32[16,256]{1,0:T(8,128)} %param.9) | copy-start | bytes 49156
  11.1 90.0 %all-to-all-start = ((bf16[4,48,4096]{2,0,1:T(4,128)(2,1)}), bf16[4,48,4096]{2,0,1:T(4,128)(2,1)S(1)}, u32[]{:S(2)}, u32[]{:S(2)}) async-start(bf16[4,48,4096]{2,0,1:T(4,128)(2,1)} %copy.9), calls=%async_computation | async-start | bytes 3145728 | tf_op jit(solution)/shard_map/all_to_all | solution.py:25
  27.6 823.4 %all-reduce.3.cloned.1.call-start = ((), (), s32[]{:S(2)}) async-start(), calls=%async_computation.2 | async-start | bytes 1572864
Sparse Core Ops, SparseCore 0:
  11.1 261.3 all-gather.1
  280.0 571.0 all-reduce.2
where the time goes:
time: 860 us; the launch traced here: 859 us
  waiting for transfers between devices  810 us (94%)
  starting transfers between devices  16.6 us (2%)
  between operations  14.2 us (2%)
  matrix products  8.97 us (1%)
    unnamed x3, waiting for transfers between devices  570 us
    all_gather x1, waiting for transfers between devices, per_device(): lax.all_gather(integrals, 'blk', axis=0, tiled=True)  170 us
    all_to_all x1, waiting for transfers between devices, per_device(): lax.all_to_all(amplitudes, 'pairs', split_axis=1, concat_axis=0, tiled=True)  69.3 us
  transfers between devices with their start and end apart: 3, of which 3 were waited for; matrix products, arithmetic and copies ran while one was open for 1% of the time, Pallas kernels for 0%

commit v1 on v0

v1 whole, which is shorter than its diff:
```python
import functools

import jax
import jax.numpy as jnp
from jax import lax
from jax.experimental import pallas as pl
from jax.experimental.pallas import tpu as pltpu
from jax.sharding import Mesh
from jax.sharding import PartitionSpec as P

TILE = 64
NOCC = 200
OT = (NOCC + TILE - 1) // TILE
ZH, Y, ZL, X, CORE = 2, 8, 6, 4, 2
PIECES = 2
ALL = ("zh", "y", "zl", "x", "c")


def onehot(index_list, width):
    return (index_list[:, None] == jnp.arange(width, dtype=jnp.int32)[None, :]).astype(jnp.bfloat16)


def split_rows(where_ref, slab_ref, pattern_ref, b_ref, *outs):
    slab = slab_ref[where_ref[1]]
    keep = pattern_ref[where_ref[0], slab].astype(jnp.float32).astype(jnp.bfloat16)
    rows = outs[0].shape[1]
    width = outs[0].shape[2]
    for piece, out in enumerate(outs):
        for y in range(Y):
            out[y] = b_ref[piece * rows : (piece + 1) * rows, y * width : (y + 1) * width] * keep


def ladder_piece(core_ref, a_ref, b_ref, mine_ref, other_ref, acc):
    step = pl.program_id(0)
    core = core_ref[0]
    half = b_ref.shape[2]

    @pl.when(step == 0)
    def _():
        acc[...] = jnp.zeros_like(acc)

    for t in range(2):
        a = a_ref[core if t == 0 else 1 - core]
        for zh in range(ZH):
            acc[t, :, zh * half : (zh + 1) * half] += lax.dot_general(
                a, b_ref[zh, 0], (((1,), (1,)), ((), ())), preferred_element_type=jnp.float32
            )

    @pl.when(step == ZL - 1)
    def _():
        columns = acc.shape[2] // 128
        chips = Y * X
        per = acc.shape[1] // chips
        for t, out in enumerate((mine_ref, other_ref)):
            for i in range(per):
                for k in range(columns):
                    out[pl.ds(i * columns + k, chips, stride=per * columns), :] = acc[
                        t, i * chips : (i + 1) * chips, k * 128 : (k + 1) * 128
                    ]


def per_device(amplitudes, integrals, amp_pattern, int_pattern, slab_ids, pair_window):
    zh, y, zl, x, c = (lax.axis_index(name) for name in ALL)
    block = zh * Y + y
    owner = (zl * X + x) * CORE + c
    pairs, slabs, depth = amplitudes.shape
    rows = integrals.shape[0]
    width = depth // Y
    part = rows // PIECES
    smem = pl.BlockSpec(memory_space=pltpu.SMEM)

    pieces = pl.pallas_call(
        split_rows,
        out_shape=[jax.ShapeDtypeStruct((Y, part, width), jnp.bfloat16)] * PIECES,
        in_specs=[smem, smem, smem, pl.BlockSpec(memory_space=pltpu.VMEM)],
        out_specs=[pl.BlockSpec(memory_space=pltpu.VMEM)] * PIECES,
    )(jnp.stack([block, owner]).astype(jnp.int32), slab_ids, int_pattern, integrals.reshape(rows, depth))

    spread = []
    gathered = []
    for piece in pieces:
        if spread:
            piece, _ = lax.optimization_barrier((piece, spread[-1]))
        moved = lax.all_to_all(piece, "y", 0, 0, tiled=True)
        spread.append(moved)
        gathered.append(lax.all_gather(moved.reshape(Y * part, width), ("zh", "zl"), axis=0, tiled=True))

    window = lax.dynamic_slice_in_dim(pair_window, (block * (ZL * X * CORE) + owner) * pairs, pairs, 1)
    occ_tile = window[0] // TILE * OT + window[1] // TILE
    picked = jnp.dot(onehot(occ_tile, amp_pattern.shape[0]), amp_pattern.astype(jnp.bfloat16))
    mask = jnp.dot(picked, onehot(slab_ids, amp_pattern.shape[1]).T)
    masked = amplitudes * mask[:, :, None]
    masked = masked.reshape(pairs, ZL, X * CORE, Y, width).transpose(3, 2, 0, 1, 4)
    masked = masked.reshape(Y * X * CORE, pairs * ZL, width)
    masked, _ = lax.optimization_barrier((masked, spread[-1]))
    swapped = lax.all_to_all(masked, ("y", "x", "c"), 0, 0, tiled=True)
    amps = swapped.reshape(Y * X, CORE, pairs, ZL, width).transpose(1, 2, 0, 3, 4)
    amps = amps.reshape(CORE, pairs * Y * X, ZL * width)

    core = c.reshape(1).astype(jnp.int32)
    cols = ZH * Y * part
    lines = cols // 128
    out_rows = Y * X * pairs * lines
    results = []
    for full in gathered:
        mine, other = pl.pallas_call(
            ladder_piece,
            grid=(ZL,),
            out_shape=[jax.ShapeDtypeStruct((out_rows, 128), jnp.float32)] * 2,
            in_specs=[
                smem,
                pl.BlockSpec((CORE, pairs * Y * X, width), lambda k: (0, 0, k)),
                pl.BlockSpec((ZH, 1, Y * part, width), lambda k: (0, k, 0, 0)),
            ],
            out_specs=[pl.BlockSpec((out_rows, 128), lambda k: (0, 0))] * 2,
            scratch_shapes=[pltpu.VMEM((2, pairs * Y * X, cols), jnp.float32)],
            compiler_params=pltpu.CompilerParams(
                dimension_semantics=("arbitrary",), vmem_limit_bytes=24 * 1024 * 1024
            ),
            cost_estimate=pl.CostEstimate(
                flops=4 * pairs * Y * X * cols * ZL * width,
                bytes_accessed=4 * 1024 * 1024,
                transcendentals=0,
            ),
        )(core, amps, full.reshape(ZH, ZL, Y * part, width))
        got = lax.ppermute(other, "c", [(0, 1), (1, 0)])
        summed = (mine + got).reshape(Y * X, pairs * lines, 128)
        sums = lax.all_to_all(summed, ("y", "x"), 0, 0, tiled=True)
        results.append(sums.sum(0).reshape(pairs, ZH * Y, part))
    return jnp.stack(results, axis=2).reshape(pairs, ZH * Y * rows)


def solution(mesh):
    fine = Mesh(mesh.devices.reshape(ZH, Y, ZL, X, CORE), ALL)
    first = ("zh", "y", "zl", "x", "c")
    placed = (P(first, None, None), P(("zh", "y"), ("zl", "x", "c"), None), P(), P(), P(), P())
    return jax.shard_map(per_device, mesh=fine, in_specs=placed, out_specs=P(first, None), check_vma=False)
```

time: 860 us -> 199 us (0.23)
  waiting for transfers between devices: 810 us -> 51.8 us
  blocking collectives: 0 us -> 81.9 us
  starting transfers between devices: 16.6 us -> 26.4 us
  Pallas kernels: 0 us -> 8.96 us
  matrix products: 8.97 us -> 0.29 us
    unnamed x3 -> x2, waiting for transfers between devices: 570 us -> 0.03 us
    all_gather x1 -> x2, waiting for transfers between devices: 170 us -> 38.1 us  [per_device(): lax.all_gather(moved.reshape(Y * part, width), ('zh', 'zl'), axis=0, tile...]
    all_to_all x0 -> x3, blocking collectives: none -> 81.9 us  [the longest x1 51.5 us: per_device(): swapped = lax.all_to_all(masked, ('y', 'x', 'c'), 0, 0, tiled=True)]
    all_to_all x1 -> x2, waiting for transfers between devices: 69.3 us -> 11.4 us  [per_device(): sums = lax.all_to_all(summed, ('y', 'x'), 0, 0, tiled=True)]
    ppermute x0 -> x2, starting transfers between devices: none -> 12.6 us  [per_device(): got = lax.ppermute(other, 'c', [(0, 1), (1, 0)])]
    pallas_call x0 -> x3, Pallas kernels: none -> 8.96 us  [the longest x2 7.07 us: per_device(): pl.pallas_call(ladder_piece, grid=(ZL,), out_shape=[jax.ShapeDtypeStruct(...]
    dot_general x5 -> x1, matrix products: 8.97 us -> 0.29 us  [per_device(): mask = jnp.dot(picked, onehot(slab_ids, amp_pattern.shape[1]).T)]
  transfers between devices with their start and end apart: 3 -> 6, of which waited for: 3 -> 4; matrix products, arithmetic and copies ran while one was open for 1% -> 5% of each run, Pallas kernels for 0% -> 4%
where the time goes in v1:
time: 199 us; the launch traced here: 198 us
  blocking collectives  81.9 us (41%)
  waiting for transfers between devices  51.8 us (26%)
  starting transfers between devices  26.4 us (13%)
  between operations  13.6 us (7%)
  local copies, waits for them, and re-layouts  12.6 us (6%)
  Pallas kernels  8.96 us (5%)
  other arithmetic  2.49 us (1%)
    all_to_all x1, blocking collectives, per_device(): swapped = lax.all_to_all(masked, ('y', 'x', 'c'), 0, 0, tiled=True)  51.5 us
    all_gather x2, waiting for transfers between devices, per_device(): lax.all_gather(moved.reshape(Y * part, width), ('zh', 'zl'), axis=0, tile...  38.1 us
    all_to_all x2, blocking collectives, per_device(): moved = lax.all_to_all(piece, 'y', 0, 0, tiled=True)  30.4 us
    all_to_all x2, starting transfers between devices, per_device(): sums = lax.all_to_all(summed, ('y', 'x'), 0, 0, tiled=True)  13.7 us
    ppermute x2, starting transfers between devices, per_device(): got = lax.ppermute(other, 'c', [(0, 1), (1, 0)])  12.6 us
    all_to_all x2, waiting for transfers between devices, per_device(): sums = lax.all_to_all(summed, ('y', 'x'), 0, 0, tiled=True)  11.4 us
    pallas_call x2, Pallas kernels, per_device(): pl.pallas_call(ladder_piece, grid=(ZL,), out_shape=[jax.ShapeDtypeStruct(...  7.07 us
  transfers between devices with their start and end apart: 6, of which 4 were waited for; matrix products, arithmetic and copies ran while one was open for 5% of the time, Pallas kernels for 4%

profile of v1, /device:TPU:1, one launch (start us, length us, event | category | flops | bytes accessed | tf_op | source)
XLA Modules:
  0.0 198.1 jit_solution(6271056862954739869)
XLA Ops:
  6.6 0.7 pad_add_fusion.where_ref
  7.3 1.9 shard_map.64
  9.2 17.1 %all_to_all.25 = bf16[8,32,512]{2,1,0:T(8,128)(2,1)} all-to-all(bf16[8,32,512]{2,1,0:T(8,128)(2,1)} %get-tuple-element.14), channel_id=1, replica_groups=mesh['zh'=2,'y'=8,'zl'=6,'x'=4,'c'=2] {'y'}, dimensions={0} | all-to-all | bytes 524288 | tf_op jit(solution)/shard_map/all_to_all | solution.py:84
  26.3 0.0 all-gather.5.cloned.1.call-start
  26.3 13.4 %all_to_all.26 = bf16[8,32,512]{2,1,0:T(8,128)(2,1)} all-to-all(bf16[8,32,512]{2,1,0:T(8,128)(2,1)} %get-tuple-element.15), channel_id=1, replica_groups=mesh['zh'=2,'y'=8,'zl'=6,'x'=4,'c'=2] {'y'}, dimensions={0} | all-to-all | bytes 524288 | tf_op jit(solution)/shard_map/all_to_all | solution.py:84
  39.7 0.1 constant_dynamic-slice_fusion
  39.8 0.3 fusion
  40.1 0.2 broadcast_multiply_fusion
  40.3 0.9 copy.11
  41.2 51.5 %all_to_all.27 = bf16[64,24,512]{2,1,0:T(8,128)(2,1)S(1)} all-to-all(bf16[64,24,512]{2,1,0:T(8,128)(2,1)S(1)} %copy.11), channel_id=1, replica_groups=mesh['zh'=2,'y'=8,'zl'=6,'x'=4,'c'=2] {'y','x','c'}, dimensions={0} | all-to-all | bytes 3145728 | tf_op jit(solution)/shard_map/all_to_all | solution.py:96
  92.7 0.5 copy.12
  93.2 0.6 reshape.103
  93.8 2.3 %copy.13 = bf16[2,4,32,6,512]{4,3,2,1,0:T(8,128)(2,1)} copy(bf16[2,4,32,6,512]{4,0,2,3,1:T(2,128)(2,1)S(1)} %bitcast.41) | data formatting | bytes 3145728 | tf_op jit(solution)/shard_map/transpose | solution.py:97
  96.1 3.6 %reshape.104.a_ref = bf16[2,128,3072]{2,1,0:T(8,128)(2,1)S(1)} reshape(bf16[2,4,32,6,512]{4,3,2,1,0:T(8,128)(2,1)} %copy.13) | data formatting | bytes 3145728 | tf_op jit(solution)/shard_map/reshape | solution.py:98
  99.7 1.9 copy-done.2
  101.6 3.5 %shard_map.65 = (f32[512,128]{1,0:T(8,128)S(1)}, f32[512,128]{1,0:T(8,128)S(1)}) custom-call(s32[1]{0:T(128)} %bitcast.core_ref, bf16[2,128,3072]{2,1,0:T(8,128)(2,1)S(1)} %reshape.104.a_ref, bf16[2,6,256,512]{3,2,1,0:T(8,128)(2,1)S(1)} %bitcast.39), custom_call_target="tpu_custom_call" | custom-call | flops 805306368 | bytes 4194304 | tf_op jit(solution)/shard_map/pallas_call | solution.py:106
  105.1 3.5 %collective-permute-start = (f32[512,128]{1,0:T(8,128)S(1)}, f32[512,128]{1,0:T(8,128)S(1)}, u32[]{:S(2)}, u32[]{:S(2)}) collective-permute-start(f32[512,128]{1,0:T(8,128)S(1)} %get-tuple-element.18), channel_id=1, source_target_pairs={{0,1},{1,0},{2,3},{3,2},{4,5},{5,4},{6,7},{7,6},{8,9},{9,8},{10,11... | collective-permute-start | bytes 786440 | tf_op jit(solution)/shard_map/ppermute | solution.py:126
  108.6 1.1 collective-permute-done
  109.7 0.7 add.44
  110.5 4.4 %all-to-all-start.3 = ((f32[32,16,128]{2,1,0:T(8,128)}), f32[32,16,128]{2,1,0:T(8,128)S(1)}, u32[]{:S(2)}, u32[]{:S(2)}) async-start(f32[32,16,128]{2,1,0:T(8,128)} %bitcast.12), calls=%async_computation.3 | async-start | bytes 524288 | tf_op jit(solution)/shard_map/all_to_all | solution.py:128
  114.9 38.0 %all-gather.5.cloned.1.call-done = bf16[3072,512]{1,0:T(8,128)(2,1)} async-done(((bf16[256,512]{1,0:T(8,128)(2,1)}), bf16[3072,512]{1,0:T(8,128)(2,1)}) %all-gather.5.cloned.1.call-update) | async-done | bytes 3145744 | tf_op jit(solution)/shard_map/all_gather | solution.py:86
  153.0 1.9 copy-done.1
  154.9 3.5 %shard_map.66 = (f32[512,128]{1,0:T(8,128)S(1)}, f32[512,128]{1,0:T(8,128)S(1)}) custom-call(s32[1]{0:T(128)} %bitcast.core_ref, bf16[2,128,3072]{2,1,0:T(8,128)(2,1)S(1)} %reshape.104.a_ref, bf16[2,6,256,512]{3,2,1,0:T(8,128)(2,1)S(1)} %bitcast.38), custom_call_target="tpu_custom_call" | custom-call | flops 805306368 | bytes 4194304 | tf_op jit(solution)/shard_map/pallas_call | solution.py:106
  158.4 9.2 %collective-permute-start.1 = (f32[512,128]{1,0:T(8,128)S(1)}, f32[512,128]{1,0:T(8,128)S(1)}, u32[]{:S(2)}, u32[]{:S(2)}) collective-permute-start(f32[512,128]{1,0:T(8,128)S(1)} %get-tuple-element.20), channel_id=1, source_target_pairs={{0,1},{1,0},{2,3},{3,2},{4,5},{5,4},{6,7},{7,6},{8,9},{9,8},{10,11... | collective-permute-start | bytes 786440 | tf_op jit(solution)/shard_map/ppermute | solution.py:126
  167.6 1.1 collective-permute-done.1
  168.7 0.7 add.45
  169.4 9.3 %all-to-all-start.4 = ((f32[32,16,128]{2,1,0:T(8,128)}), f32[32,16,128]{2,1,0:T(8,128)S(1)}, u32[]{:S(2)}, u32[]{:S(2)}) async-start(f32[32,16,128]{2,1,0:T(8,128)} %bitcast.15), calls=%async_computation.4 | async-start | bytes 524288 | tf_op jit(solution)/shard_map/all_to_all | solution.py:128
  178.8 0.1 stack_reshape.6
  178.9 11.4 %all-to-all-done.4 = f32[32,16,128]{2,1,0:T(8,128)S(1)} async-done(((f32[32,16,128]{2,1,0:T(8,128)}), f32[32,16,128]{2,1,0:T(8,128)S(1)}, u32[]{:S(2)}, u32[]{:S(2)}) %all-to-all-start.4) | async-done | bytes 262176 | tf_op jit(solution)/shard_map/all_to_all | solution.py:128
  190.3 0.1 stack_reshape.7
  190.4 0.1 pad_maximum_fusion
  190.5 0.7 reshape.111
  (18 shorter events, 0.2 us)
Async XLA Ops:
  6.5 33.2 %copy-start = (s32[2,3072]{1,0:T(2,128)S(1)}, s32[2,3072]{1,0:T(2,128)}, u32[]{:S(2)}) copy-start(s32[2,3072]{1,0:T(2,128)} %param.11) | copy-start | bytes 73732
  6.5 33.3 %copy-start.4 = (s32[48]{0:T(128)S(1)}, s32[48]{0:T(128)}, u32[]{:S(2)}) copy-start(s32[48]{0:T(128)} %slab_ref.1) | copy-start | bytes 580
  6.5 33.3 %copy-start.5 = (s32[16,256]{1,0:T(8,128)S(1)}, s32[16,256]{1,0:T(8,128)}, u32[]{:S(2)}) copy-start(s32[16,256]{1,0:T(8,128)} %param.8) | copy-start | bytes 49156
  6.5 33.6 %copy-start.3 = (bf16[4,48,4096]{2,1,0:T(8,128)(2,1)S(1)}, bf16[4,48,4096]{2,1,0:T(8,128)(2,1)}, u32[]{:S(2)}) copy-start(bf16[4,48,4096]{2,1,0:T(8,128)(2,1)} %param.6) | copy-start | bytes 4718596
  6.5 93.1 %all-gather.3.cloned.1.call-start = ((), (), s32[]{:S(2)}) async-start(), calls=%async_computation.5 | async-start | bytes 3407872 | tf_op jit(solution)/shard_map/all_gather | solution.py:86
  26.3 126.7 %all-gather.5.cloned.1.call-start = ((), (), s32[]{:S(2)}) async-start(), calls=%async_computation.6 | async-start | bytes 3407872 | tf_op jit(solution)/shard_map/all_gather | solution.py:86
  99.7 1.9 copy-start.2
  105.1 4.6 %collective-permute-start = (f32[512,128]{1,0:T(8,128)S(1)}, f32[512,128]{1,0:T(8,128)S(1)}, u32[]{:S(2)}, u32[]{:S(2)}) collective-permute-start(f32[512,128]{1,0:T(8,128)S(1)} %get-tuple-element.18), channel_id=1, source_target_pairs={{0,1},{1,0},{2,3},{3,2},{4,5},{5,4},{6,7},{7,6},{8,9},{9,8},{10,11... | collective-permute-start | bytes 786440 | tf_op jit(solution)/shard_map/ppermute | solution.py:126
  110.5 59.0 %all-to-all-start.3 = ((f32[32,16,128]{2,1,0:T(8,128)}), f32[32,16,128]{2,1,0:T(8,128)S(1)}, u32[]{:S(2)}, u32[]{:S(2)}) async-start(f32[32,16,128]{2,1,0:T(8,128)} %bitcast.12), calls=%async_computation.3 | async-start | bytes 524288 | tf_op jit(solution)/shard_map/all_to_all | solution.py:128
  153.0 1.9 copy-start.1
  158.4 10.3 %collective-permute-start.1 = (f32[512,128]{1,0:T(8,128)S(1)}, f32[512,128]{1,0:T(8,128)S(1)}, u32[]{:S(2)}, u32[]{:S(2)}) collective-permute-start(f32[512,128]{1,0:T(8,128)S(1)} %get-tuple-element.20), channel_id=1, source_target_pairs={{0,1},{1,0},{2,3},{3,2},{4,5},{5,4},{6,7},{7,6},{8,9},{9,8},{10,11... | collective-permute-start | bytes 786440 | tf_op jit(solution)/shard_map/ppermute | solution.py:126
  169.4 20.9 %all-to-all-start.4 = ((f32[32,16,128]{2,1,0:T(8,128)}), f32[32,16,128]{2,1,0:T(8,128)S(1)}, u32[]{:S(2)}, u32[]{:S(2)}) async-start(f32[32,16,128]{2,1,0:T(8,128)} %bitcast.15), calls=%async_computation.4 | async-start | bytes 524288 | tf_op jit(solution)/shard_map/all_to_all | solution.py:128
Sparse Core Ops, SparseCore 0:
  26.4 62.3 all-gather.2
  91.2 61.7 all-gather.4

commit v2 on v1

v2 whole, which is shorter than its diff:
```python
import functools

import jax
import jax.numpy as jnp
from jax import lax
from jax.experimental import pallas as pl
from jax.experimental.pallas import tpu as pltpu
from jax.sharding import Mesh
from jax.sharding import PartitionSpec as P

TILE = 64
NOCC = 200
OT = (NOCC + TILE - 1) // TILE
ZH, Y, ZL, X, CORE = 2, 8, 6, 4, 2
ALL = ("zh", "y", "zl", "x", "c")


def onehot(index_list, width):
    return (index_list[:, None] == jnp.arange(width, dtype=jnp.int32)[None, :]).astype(jnp.bfloat16)


def split_depth(where_ref, slab_ref, pattern_ref, b_ref, out):
    slab = slab_ref[where_ref[1]]
    keep = pattern_ref[where_ref[0], slab].astype(jnp.float32).astype(jnp.bfloat16)
    width = out.shape[2]
    for y in range(Y):
        out[y] = b_ref[:, y * width : (y + 1) * width] * keep


def ladder_core(core_ref, a_ref, b_ref, out, acc):
    step = pl.program_id(0)
    a = a_ref[core_ref[0]]
    half = b_ref.shape[2]

    @pl.when(step == 0)
    def _():
        acc[...] = jnp.zeros_like(acc)

    for zh in range(ZH):
        acc[:, zh * half : (zh + 1) * half] += lax.dot_general(
            a, b_ref[zh, 0], (((1,), (1,)), ((), ())), preferred_element_type=jnp.float32
        )

    @pl.when(step == ZL - 1)
    def _():
        columns = acc.shape[1] // 128
        chips = Y * X
        per = acc.shape[0] // chips
        for i in range(per):
            for k in range(columns):
                out[pl.ds(i * columns + k, chips, stride=per * columns), :] = acc[
                    i * chips : (i + 1) * chips, k * 128 : (k + 1) * 128
                ]


def per_device(amplitudes, integrals, amp_pattern, int_pattern, slab_ids, pair_window):
    zh, y, zl, x, c = (lax.axis_index(name) for name in ALL)
    block = zh * Y + y
    owner = (zl * X + x) * CORE + c
    pairs, slabs, depth = amplitudes.shape
    rows = integrals.shape[0]
    width = depth // Y
    smem = pl.BlockSpec(memory_space=pltpu.SMEM)

    ready = pl.pallas_call(
        split_depth,
        out_shape=jax.ShapeDtypeStruct((Y, rows, width), jnp.bfloat16),
        in_specs=[smem, smem, smem, pl.BlockSpec(memory_space=pltpu.VMEM)],
        out_specs=pl.BlockSpec(memory_space=pltpu.VMEM),
    )(jnp.stack([block, owner]).astype(jnp.int32), slab_ids, int_pattern, integrals.reshape(rows, depth))
    moved = lax.all_to_all(ready, "y", 0, 0, tiled=True)
    gathered = lax.all_gather(moved.reshape(Y * rows, width), ("zh", "zl"), axis=0, tiled=True)
    gathered = gathered.reshape(ZH, ZL, Y * rows, width)

    window = lax.dynamic_slice_in_dim(pair_window, (block * (ZL * X * CORE) + owner) * pairs, pairs, 1)
    occ_tile = window[0] // TILE * OT + window[1] // TILE
    picked = jnp.dot(onehot(occ_tile, amp_pattern.shape[0]), amp_pattern.astype(jnp.bfloat16))
    mask = jnp.dot(picked, onehot(slab_ids, amp_pattern.shape[1]).T)
    masked = amplitudes * mask[:, :, None]
    masked = masked.reshape(pairs, ZL, X * CORE, Y, width).transpose(3, 2, 0, 1, 4)
    masked = masked.reshape(Y * X * CORE, pairs * ZL, width)
    masked, _ = lax.optimization_barrier((masked, moved))
    swapped = lax.all_to_all(masked, ("y", "x", "c"), 0, 0, tiled=True)
    amps = swapped.reshape(Y * X, CORE, pairs, ZL, width).transpose(1, 2, 0, 3, 4)
    amps = amps.reshape(CORE, pairs * Y * X, ZL * width)

    cols = ZH * Y * rows
    lines = cols // 128
    out_rows = Y * X * pairs * lines

    def product(core, amps):
        return pl.pallas_call(
            ladder_core,
            grid=(ZL,),
            out_shape=jax.ShapeDtypeStruct((out_rows, 128), jnp.float32),
            in_specs=[
                smem,
                pl.BlockSpec((CORE, pairs * Y * X, width), lambda k: (0, 0, k)),
                pl.BlockSpec((ZH, 1, Y * rows, width), lambda k: (0, k, 0, 0)),
            ],
            out_specs=pl.BlockSpec((out_rows, 128), lambda k: (0, 0)),
            scratch_shapes=[pltpu.VMEM((pairs * Y * X, cols), jnp.float32)],
            compiler_params=pltpu.CompilerParams(
                dimension_semantics=("arbitrary",), vmem_limit_bytes=56 * 1024 * 1024
            ),
            cost_estimate=pl.CostEstimate(
                flops=2 * pairs * Y * X * cols * ZL * width,
                bytes_accessed=8 * 1024 * 1024,
                transcendentals=0,
            ),
        )(core.reshape(1).astype(jnp.int32), amps, gathered)

    other = product(1 - c, amps)
    got = lax.ppermute(other, "c", [(0, 1), (1, 0)])
    later, _ = lax.optimization_barrier((amps, other))
    mine = product(c, later)
    summed = (mine + got).reshape(Y * X, pairs * lines, 128)
    sums = lax.all_to_all(summed, ("y", "x"), 0, 0, tiled=True)
    return sums.sum(0).reshape(pairs, cols)


def solution(mesh):
    fine = Mesh(mesh.devices.reshape(ZH, Y, ZL, X, CORE), ALL)
    first = ("zh", "y", "zl", "x", "c")
    placed = (P(first, None, None), P(("zh", "y"), ("zl", "x", "c"), None), P(), P(), P(), P())
    return jax.shard_map(per_device, mesh=fine, in_specs=placed, out_specs=P(first, None), check_vma=False)
```

time: 199 us -> 173 us (0.87)
  blocking collectives: 81.9 us -> 45.8 us
  waiting for transfers between devices: 51.8 us -> 69.3 us
  starting transfers between devices: 26.4 us -> 14.7 us
  Pallas kernels: 8.96 us -> 16.7 us
  local copies, waits for them, and re-layouts: 12.6 us -> 10.4 us
    all_to_all x3 -> x2, blocking collectives: 81.9 us -> 45.8 us  [the longest x1 25.9 us: per_device(): sums = lax.all_to_all(summed, ('y', 'x'), 0, 0, tiled=True)]
    all_to_all x2 -> x1, waiting for transfers between devices: 11.4 us -> 39.1 us  [per_device(): swapped = lax.all_to_all(masked, ('y', 'x', 'c'), 0, 0, tiled=True)]
    ppermute x2 -> x1, starting transfers between devices: 12.6 us -> 2.58 us  [per_device(): got = lax.ppermute(other, 'c', [(0, 1), (1, 0)])]
    all_gather x2 -> x1, waiting for transfers between devices: 38.1 us -> 30.2 us  [per_device(): lax.all_gather(moved.reshape(Y * rows, width), ('zh', 'zl'), axis=0, tile...]
    pallas_call x3, Pallas kernels: 8.96 us -> 16.7 us  [the longest x2 14.8 us: product(): pl.pallas_call(ladder_core, grid=(ZL,), out_shape=jax.ShapeDtypeStruct((o...]
    unnamed x12 -> x8, local copies, waits for them, and re-layouts: 3.79 us -> 0.02 us
    ppermute x2 -> x1, waiting for transfers between devices: 2.28 us -> 0.01 us  [per_device(): got = lax.ppermute(other, 'c', [(0, 1), (1, 0)])]
    all_to_all x2 -> x1, starting transfers between devices: 13.7 us -> 12.1 us  [per_device(): swapped = lax.all_to_all(masked, ('y', 'x', 'c'), 0, 0, tiled=True)]
  transfers between devices with their start and end apart: 6 -> 3, of which waited for: 4 -> 2; matrix products, arithmetic and copies ran while one was open for 5% -> 6% of each run, Pallas kernels for 4% -> 4%
where the time goes in v2:
time: 173 us
  waiting for transfers between devices  69.3 us (40%)
  blocking collectives  45.8 us (26%)
  Pallas kernels  16.7 us (10%)
  starting transfers between devices  14.7 us (8%)
  between operations  13.5 us (8%)
  local copies, waits for them, and re-layouts  10.4 us (6%)
  other arithmetic  1.97 us (1%)
    all_to_all x1, waiting for transfers between devices, per_device(): swapped = lax.all_to_all(masked, ('y', 'x', 'c'), 0, 0, tiled=True)  39.1 us
    all_gather x1, waiting for transfers between devices, per_device(): lax.all_gather(moved.reshape(Y * rows, width), ('zh', 'zl'), axis=0, tile...  30.2 us
    all_to_all x1, blocking collectives, per_device(): sums = lax.all_to_all(summed, ('y', 'x'), 0, 0, tiled=True)  25.9 us
    all_to_all x1, blocking collectives, per_device(): moved = lax.all_to_all(ready, 'y', 0, 0, tiled=True)  19.9 us
    pallas_call x2, Pallas kernels, product(): pl.pallas_call(ladder_core, grid=(ZL,), out_shape=jax.ShapeDtypeStruct((o...  14.8 us
    all_to_all x1, starting transfers between devices, per_device(): swapped = lax.all_to_all(masked, ('y', 'x', 'c'), 0, 0, tiled=True)  12.1 us
  transfers between devices with their start and end apart: 3, of which 2 were waited for; matrix products, arithmetic and copies ran while one was open for 6% of the time, Pallas kernels for 4%

profile of v2, /device:TPU:1, one launch (start us, length us, event | category | flops | bytes accessed | tf_op | source)
XLA Modules:
  0.0 172.7 jit_solution(11447407173159975669)
XLA Ops:
  6.5 0.0 copy-start
  6.5 0.0 copy-start.2
  6.5 0.0 copy-start.3
  6.5 0.0 copy-start.1
  6.5 0.0 all-gather.2.cloned.1.call-start
  6.6 0.6 pad_add_fusion.where_ref
  7.2 1.9 %shard_map.64 = bf16[8,64,512]{2,1,0:T(8,128)(2,1)} custom-call(s32[2]{0:T(128)} %pad_add_fusion.where_ref, s32[48]{0:T(128)} %slab_ref.1, s32[16,256]{1,0:T(8,128)} %pattern_ref.1, bf16[64,4096]{1,0:T(8,128)(2,1)} %bitcast.42), custom_call_target="tpu_custom_call" | custom-call | tf_op jit(solution)/shard_map/pallas_call | solution.py:65
  9.1 19.9 %all_to_all.15 = bf16[8,64,512]{2,1,0:T(8,128)(2,1)} all-to-all(bf16[8,64,512]{2,1,0:T(8,128)(2,1)} %shard_map.64), channel_id=1, replica_groups=mesh['zh'=2,'y'=8,'zl'=6,'x'=4,'c'=2] {'y'}, dimensions={0} | all-to-all | bytes 1048576 | tf_op jit(solution)/shard_map/all_to_all | solution.py:71
  29.0 0.0 all-gather.2.cloned.1.call-update
  29.0 0.0 copy-done
  29.0 0.1 constant_dynamic-slice_fusion
  29.1 0.0 copy-done.2
  29.1 0.0 copy-done.3
  29.2 0.3 fusion
  29.5 0.0 copy-done.1
  29.5 0.2 broadcast_multiply_fusion
  29.6 2.0 %copy.11 = bf16[64,24,512]{2,1,0:T(8,128)(2,1)} copy(bf16[64,24,512]{2,0,1:T(8,128)(2,1)S(1)} %bitcast.38) | data formatting | bytes 3145728 | tf_op jit(solution)/shard_map/optimization_barrier | solution.py:82
  31.6 12.1 %all-to-all-start.1 = ((bf16[64,24,512]{2,1,0:T(8,128)(2,1)}), bf16[64,24,512]{2,1,0:T(8,128)(2,1)S(1)}, u32[]{:S(2)}, u32[]{:S(2)}) async-start(bf16[64,24,512]{2,1,0:T(8,128)(2,1)} %copy.11), calls=%async_computation.1 | async-start | bytes 3145728 | tf_op jit(solution)/shard_map/all_to_all | solution.py:83
  43.8 39.1 %all-to-all-done.1 = bf16[64,24,512]{2,1,0:T(8,128)(2,1)S(1)} async-done(((bf16[64,24,512]{2,1,0:T(8,128)(2,1)}), bf16[64,24,512]{2,1,0:T(8,128)(2,1)S(1)}, u32[]{:S(2)}, u32[]{:S(2)}) %all-to-all-start.1) | async-done | bytes 1572896 | tf_op jit(solution)/shard_map/all_to_all | solution.py:83
  82.9 0.5 copy.12
  83.4 2.0 %reshape.97 = bf16[32,2,4,6,512]{4,1,0,3,2:T(2,128)(2,1)} reshape(bf16[64,24,512]{2,0,1:T(8,128)(2,1)S(1)} %copy.12) | data formatting | bytes 3145728 | tf_op jit(solution)/shard_map/reshape | solution.py:84
  85.4 2.4 %copy.13 = bf16[2,4,32,6,512]{4,3,2,1,0:T(8,128)(2,1)S(1)} copy(bf16[2,4,32,6,512]{4,0,2,3,1:T(2,128)(2,1)} %bitcast.39) | data formatting | bytes 3145728 | tf_op jit(solution)/shard_map/transpose | solution.py:84
  87.8 2.8 %reshape.98.a_ref = bf16[2,128,3072]{2,1,0:T(8,128)(2,1)} reshape(bf16[2,4,32,6,512]{4,3,2,1,0:T(8,128)(2,1)S(1)} %copy.13) | data formatting | bytes 3145728 | tf_op jit(solution)/shard_map/reshape | solution.py:85
  90.6 30.2 %all-gather.2.cloned.1.call-done = bf16[6144,512]{1,0:T(8,128)(2,1)} async-done(((bf16[512,512]{1,0:T(8,128)(2,1)}), bf16[6144,512]{1,0:T(8,128)(2,1)}) %all-gather.2.cloned.1.call-update) | async-done | bytes 6291472 | tf_op jit(solution)/shard_map/all_gather | solution.py:72
  120.8 7.4 %shard_map.65 = f32[1024,128]{1,0:T(8,128)} custom-call(s32[1]{0:T(128)} %bitcast.10.core_ref, bf16[2,128,3072]{2,1,0:T(8,128)(2,1)} %reshape.98.a_ref, bf16[2,6,512,512]{3,2,1,0:T(8,128)(2,1)} %bitcast.36), custom_call_target="tpu_custom_call" | custom-call | flops 805306368 | bytes 8388608 | tf_op jit(solution)/shard_map/pallas_call | solution.py:92
  128.2 2.6 %collective-permute-start = (f32[1024,128]{1,0:T(8,128)}, f32[1024,128]{1,0:T(8,128)S(1)}, u32[]{:S(2)}, u32[]{:S(2)}) collective-permute-start(f32[1024,128]{1,0:T(8,128)} %shard_map.65), channel_id=1, source_target_pairs={{0,1},{1,0},{2,3},{3,2},{4,5},{5,4},{6,7},{7,6},{8,9},{9,8},{10,11... | collective-permute-start | bytes 1572872 | tf_op jit(solution)/shard_map/ppermute | solution.py:114
  130.8 7.4 %shard_map.66 = f32[1024,128]{1,0:T(8,128)} custom-call(s32[1]{0:T(128)} %bitcast.core_ref, bf16[2,128,3072]{2,1,0:T(8,128)(2,1)} %reshape.98.a_ref, bf16[2,6,512,512]{3,2,1,0:T(8,128)(2,1)} %bitcast.37), custom_call_target="tpu_custom_call" | custom-call | flops 805306368 | bytes 8388608 | tf_op jit(solution)/shard_map/pallas_call | solution.py:92
  138.2 0.0 collective-permute-done
  138.2 1.1 add.41
  139.3 25.9 %all_to_all.16 = f32[32,32,128]{2,1,0:T(8,128)S(1)} all-to-all(f32[32,32,128]{2,1,0:T(8,128)S(1)} %bitcast.40), channel_id=1, replica_groups=mesh['zh'=2,'y'=8,'zl'=6,'x'=4,'c'=2] {'y','x'}, dimensions={0} | all-to-all | bytes 1048576 | tf_op jit(solution)/shard_map/all_to_all | solution.py:118
  165.2 0.6 reshape.103
  (2 shorter events, 0.1 us)
Async XLA Ops:
  6.5 22.5 %copy-start = (s32[2,3072]{1,0:T(2,128)S(1)}, s32[2,3072]{1,0:T(2,128)}, u32[]{:S(2)}) copy-start(s32[2,3072]{1,0:T(2,128)} %param.11) | copy-start | bytes 73732
  6.5 22.6 %copy-start.2 = (s32[48]{0:T(128)S(1)}, s32[48]{0:T(128)}, u32[]{:S(2)}) copy-start(s32[48]{0:T(128)} %slab_ref.1) | copy-start | bytes 580
  6.5 22.6 %copy-start.3 = (s32[16,256]{1,0:T(8,128)S(1)}, s32[16,256]{1,0:T(8,128)}, u32[]{:S(2)}) copy-start(s32[16,256]{1,0:T(8,128)} %param.8) | copy-start | bytes 49156
  6.5 22.9 %copy-start.1 = (bf16[4,48,4096]{2,1,0:T(8,128)(2,1)S(1)}, bf16[4,48,4096]{2,1,0:T(8,128)(2,1)}, u32[]{:S(2)}) copy-start(bf16[4,48,4096]{2,1,0:T(8,128)(2,1)} %param.6) | copy-start | bytes 4718596
  6.5 114.2 %all-gather.2.cloned.1.call-start = ((), (), s32[]{:S(2)}) async-start(), calls=%async_computation.3 | async-start | bytes 6815744 | tf_op jit(solution)/shard_map/all_gather | solution.py:72
  31.6 51.2 %all-to-all-start.1 = ((bf16[64,24,512]{2,1,0:T(8,128)(2,1)}), bf16[64,24,512]{2,1,0:T(8,128)(2,1)S(1)}, u32[]{:S(2)}, u32[]{:S(2)}) async-start(bf16[64,24,512]{2,1,0:T(8,128)(2,1)} %copy.11), calls=%async_computation.1 | async-start | bytes 3145728 | tf_op jit(solution)/shard_map/all_to_all | solution.py:83
  128.2 10.0 %collective-permute-start = (f32[1024,128]{1,0:T(8,128)}, f32[1024,128]{1,0:T(8,128)S(1)}, u32[]{:S(2)}, u32[]{:S(2)}) collective-permute-start(f32[1024,128]{1,0:T(8,128)} %shard_map.65), channel_id=1, source_target_pairs={{0,1},{1,0},{2,3},{3,2},{4,5},{5,4},{6,7},{7,6},{8,9},{9,8},{10,11... | collective-permute-start | bytes 1572872 | tf_op jit(solution)/shard_map/ppermute | solution.py:114
Sparse Core Ops, SparseCore 0:
  29.1 91.5 all-gather.1

commit v3 on v2

--- a/solution.py
+++ b/solution.py
@@ -27,30 +27,40 @@
         out[y] = b_ref[:, y * width : (y + 1) * width] * keep
 
 
-def ladder_core(core_ref, a_ref, b_ref, out, acc):
-    step = pl.program_id(0)
-    a = a_ref[core_ref[0]]
-    half = b_ref.shape[2]
-
-    @pl.when(step == 0)
-    def _():
-        acc[...] = jnp.zeros_like(acc)
-
-    for zh in range(ZH):
-        acc[:, zh * half : (zh + 1) * half] += lax.dot_general(
-            a, b_ref[zh, 0], (((1,), (1,)), ((), ())), preferred_element_type=jnp.float32
+def ladder(core_ref, a_ref, b_ref, mine_ref, other_ref, held, landed):
+    core = core_ref[0]
+    width = b_ref.shape[3]
+    copies = [
+        [
+            pltpu.make_async_copy(
+                b_ref.at[zh, zl], held.at[zh, :, pl.ds(zl * width, width)], landed.at[zh, zl]
+            )
+            for zl in range(ZL)
+        ]
+        for zh in range(ZH)
+    ]
+    for group in copies:
+        for copy in group:
+            copy.start()
+    per = a_ref.shape[1]
+    chips = Y * X
+    stride = mine_ref.shape[0] // chips
+    columns = stride * chips // per
+    both = jnp.concatenate([a_ref[core], a_ref[1 - core]], axis=0)
+    for zh, group in enumerate(copies):
+        for copy in group:
+            copy.wait()
+        acc = lax.dot_general(
+            both, held[zh], (((1,), (1,)), ((), ())), preferred_element_type=jnp.float32
         )
-
-    @pl.when(step == ZL - 1)
-    def _():
-        columns = acc.shape[1] // 128
-        chips = Y * X
-        per = acc.shape[0] // chips
-        for i in range(per):
-            for k in range(columns):
-                out[pl.ds(i * columns + k, chips, stride=per * columns), :] = acc[
-                    i * chips : (i + 1) * chips, k * 128 : (k + 1) * 128
-                ]
+        tiles = acc.shape[1] // 128
+        for t, out in enumerate((mine_ref, other_ref)):
+            for i in range(per // chips):
+                for k in range(tiles):
+                    start = t * per + i * chips
+                    out[pl.ds(i * columns + zh * tiles + k, chips, stride=stride), :] = acc[
+                        start : start + chips, k * 128 : (k + 1) * 128
+                    ]
 
 
 def per_device(amplitudes, integrals, amp_pattern, int_pattern, slab_ids, pair_window):
@@ -88,32 +98,21 @@
     lines = cols // 128
     out_rows = Y * X * pairs * lines
 
-    def product(core, amps):
-        return pl.pallas_call(
-            ladder_core,
-            grid=(ZL,),
-            out_shape=jax.ShapeDtypeStruct((out_rows, 128), jnp.float32),
-            in_specs=[
-                smem,
-                pl.BlockSpec((CORE, pairs * Y * X, width), lambda k: (0, 0, k)),
-                pl.BlockSpec((ZH, 1, Y * rows, width), lambda k: (0, k, 0, 0)),
-            ],
-            out_specs=pl.BlockSpec((out_rows, 128), lambda k: (0, 0)),
-            scratch_shapes=[pltpu.VMEM((pairs * Y * X, cols), jnp.float32)],
-            compiler_params=pltpu.CompilerParams(
-                dimension_semantics=("arbitrary",), vmem_limit_bytes=56 * 1024 * 1024
-            ),
-            cost_estimate=pl.CostEstimate(
-                flops=2 * pairs * Y * X * cols * ZL * width,
-                bytes_accessed=8 * 1024 * 1024,
-                transcendentals=0,
-            ),
-        )(core.reshape(1).astype(jnp.int32), amps, gathered)
-
-    other = product(1 - c, amps)
+    mine, other = pl.pallas_call(
+        ladder,
+        out_shape=[jax.ShapeDtypeStruct((out_rows, 128), jnp.float32)] * 2,
+        in_specs=[smem, pl.BlockSpec(memory_space=pltpu.VMEM), pl.BlockSpec(memory_space=pltpu.HBM)],
+        out_specs=[pl.BlockSpec(memory_space=pltpu.VMEM)] * 2,
+        scratch_shapes=[
+            pltpu.VMEM((ZH, Y * rows, ZL * width), jnp.bfloat16),
+            pltpu.SemaphoreType.DMA((ZH, ZL)),
+        ],
+        compiler_params=pltpu.CompilerParams(vmem_limit_bytes=48 * 1024 * 1024),
+        cost_estimate=pl.CostEstimate(
+            flops=4 * pairs * Y * X * cols * ZL * width, bytes_accessed=8 * 1024 * 1024, transcendentals=0
+        ),
+    )(c.reshape(1).astype(jnp.int32), amps, gathered)
     got = lax.ppermute(other, "c", [(0, 1), (1, 0)])
-    later, _ = lax.optimization_barrier((amps, other))
-    mine = product(c, later)
     summed = (mine + got).reshape(Y * X, pairs * lines, 128)
     sums = lax.all_to_all(summed, ("y", "x"), 0, 0, tiled=True)
     return sums.sum(0).reshape(pairs, cols)

time: 173 us -> 163 us (0.942)
  blocking collectives: 45.8 us -> 96 us
  waiting for transfers between devices: 69.3 us -> 34.4 us
  starting transfers between devices: 14.7 us -> 2.61 us
  Pallas kernels: 16.7 us -> 6.36 us
  local copies, waits for them, and re-layouts: 10.4 us -> 8.56 us
    all_to_all x0 -> x1, blocking collectives: none -> 50.4 us  [per_device(): swapped = lax.all_to_all(masked, ('y', 'x', 'c'), 0, 0, tiled=True)]
    all_to_all x1 -> x0, waiting for transfers between devices: 39.1 us -> none  [per_device(): swapped = lax.all_to_all(masked, ('y', 'x', 'c'), 0, 0, tiled=True)]
    all_to_all x1 -> x0, starting transfers between devices: 12.1 us -> none  [per_device(): swapped = lax.all_to_all(masked, ('y', 'x', 'c'), 0, 0, tiled=True)]
    pallas_call x2 -> x1, Pallas kernels: 14.8 us -> 4.46 us  [per_device(): pl.pallas_call(ladder, out_shape=[jax.ShapeDtypeStruct((out_rows, 128), j...]
    all_gather x1, waiting for transfers between devices: 30.2 us -> 32.8 us  [per_device(): lax.all_gather(moved.reshape(Y * rows, width), ('zh', 'zl'), axis=0, tile...]
  transfers between devices with their start and end apart: 3 -> 2, of which waited for: 2 -> 2; matrix products, arithmetic and copies ran while one was open for 6% -> 5% of each run, Pallas kernels for 4% -> 0%
where the time goes in v3:
time: 163 us
  blocking collectives  96 us (59%)
  waiting for transfers between devices  34.4 us (21%)
  between operations  13.5 us (8%)
  local copies, waits for them, and re-layouts  8.56 us (5%)
  Pallas kernels  6.36 us (4%)
  starting transfers between devices  2.61 us (2%)
    all_to_all x1, blocking collectives, per_device(): swapped = lax.all_to_all(masked, ('y', 'x', 'c'), 0, 0, tiled=True)  50.4 us
    all_gather x1, waiting for transfers between devices, per_device(): lax.all_gather(moved.reshape(Y * rows, width), ('zh', 'zl'), axis=0, tile...  32.8 us
    all_to_all x1, blocking collectives, per_device(): sums = lax.all_to_all(summed, ('y', 'x'), 0, 0, tiled=True)  25.6 us
    all_to_all x1, blocking collectives, per_device(): moved = lax.all_to_all(ready, 'y', 0, 0, tiled=True)  19.9 us
    pallas_call x1, Pallas kernels, per_device(): pl.pallas_call(ladder, out_shape=[jax.ShapeDtypeStruct((out_rows, 128), j...  4.46 us
    reshape x1, local copies, waits for them, and re-layouts, per_device(): amps = amps.reshape(CORE, pairs * Y * X, ZL * width)  3.56 us
  transfers between devices with their start and end apart: 2, of which 2 were waited for; matrix products, arithmetic and copies ran while one was open for 5% of the time, Pallas kernels for 0%

profile of v3, /device:TPU:1, one launch (start us, length us, event | category | flops | bytes accessed | tf_op | source)
XLA Modules:
  0.0 162.5 jit_solution(4641504088426350637)
XLA Ops:
  6.5 0.0 copy-start
  6.5 0.0 copy-start.2
  6.5 0.0 copy-start.3
  6.5 0.0 copy-start.1
  6.5 0.0 all-gather.2.cloned.1.call-start
  6.6 0.6 pad_add_fusion.where_ref
  7.2 1.9 %shard_map.64 = bf16[8,64,512]{2,1,0:T(8,128)(2,1)} custom-call(s32[2]{0:T(128)} %pad_add_fusion.where_ref, s32[48]{0:T(128)} %slab_ref.1, s32[16,256]{1,0:T(8,128)} %pattern_ref.1, bf16[64,4096]{1,0:T(8,128)(2,1)} %bitcast.40), custom_call_target="tpu_custom_call" | custom-call | tf_op jit(solution)/shard_map/pallas_call | solution.py:75
  9.1 19.9 %all_to_all.15 = bf16[8,64,512]{2,1,0:T(8,128)(2,1)} all-to-all(bf16[8,64,512]{2,1,0:T(8,128)(2,1)} %shard_map.64), channel_id=1, replica_groups=mesh['zh'=2,'y'=8,'zl'=6,'x'=4,'c'=2] {'y'}, dimensions={0} | all-to-all | bytes 1048576 | tf_op jit(solution)/shard_map/all_to_all | solution.py:81
  29.0 0.0 all-gather.2.cloned.1.call-update
  29.0 0.0 copy-done
  29.0 0.1 constant_dynamic-slice_fusion
  29.1 0.0 copy-done.2
  29.1 0.0 copy-done.3
  29.1 0.3 fusion
  29.4 0.0 copy-done.1
  29.4 0.2 broadcast_multiply_fusion
  29.6 0.9 copy.11
  30.5 50.4 %all_to_all.16 = bf16[64,24,512]{2,1,0:T(8,128)(2,1)S(1)} all-to-all(bf16[64,24,512]{2,1,0:T(8,128)(2,1)S(1)} %copy.11), channel_id=1, replica_groups=mesh['zh'=2,'y'=8,'zl'=6,'x'=4,'c'=2] {'y','x','c'}, dimensions={0} | all-to-all | bytes 3145728 | tf_op jit(solution)/shard_map/all_to_all | solution.py:93
  80.9 0.5 copy.12
  81.4 0.6 reshape.94
  82.1 2.3 %copy.13 = bf16[2,4,32,6,512]{4,3,2,1,0:T(8,128)(2,1)} copy(bf16[2,4,32,6,512]{4,0,2,3,1:T(2,128)(2,1)S(1)} %bitcast.36) | data formatting | bytes 3145728 | tf_op jit(solution)/shard_map/transpose | solution.py:94
  84.4 3.6 %reshape.95.a_ref = bf16[2,128,3072]{2,1,0:T(8,128)(2,1)S(1)} reshape(bf16[2,4,32,6,512]{4,3,2,1,0:T(8,128)(2,1)} %copy.13) | data formatting | bytes 3145728 | tf_op jit(solution)/shard_map/reshape | solution.py:95
  87.9 32.8 %all-gather.2.cloned.1.call-done = bf16[6144,512]{1,0:T(8,128)(2,1)} async-done(((bf16[512,512]{1,0:T(8,128)(2,1)}), bf16[6144,512]{1,0:T(8,128)(2,1)}) %all-gather.2.cloned.1.call-update) | async-done | bytes 6291472 | tf_op jit(solution)/shard_map/all_gather | solution.py:82
  120.7 4.5 %shard_map.65 = (f32[1024,128]{1,0:T(8,128)S(1)}, f32[1024,128]{1,0:T(8,128)S(1)}) custom-call(s32[1]{0:T(128)} %bitcast.core_ref, bf16[2,128,3072]{2,1,0:T(8,128)(2,1)S(1)} %reshape.95.a_ref, bf16[2,6,512,512]{3,2,1,0:T(8,128)(2,1)} %bitcast.37), custom_call_target="tpu_custom_call" | custom-call | flops 1610612736 | bytes 8388608 | tf_op jit(solution)/shard_map/pallas_call | solution.py:101
  125.2 2.6 %collective-permute-start = (f32[1024,128]{1,0:T(8,128)S(1)}, f32[1024,128]{1,0:T(8,128)S(1)}, u32[]{:S(2)}, u32[]{:S(2)}) collective-permute-start(f32[1024,128]{1,0:T(8,128)S(1)} %get-tuple-element.10), channel_id=1, source_target_pairs={{0,1},{1,0},{2,3},{3,2},{4,5},{5,4},{6,7},{7,6},{8,9},{9,8},{10,11... | collective-permute-start | bytes 1572872 | tf_op jit(solution)/shard_map/ppermute | solution.py:115
  127.8 1.5 collective-permute-done
  129.3 0.1 add.41
  129.4 25.6 %all_to_all.17 = f32[32,32,128]{2,1,0:T(8,128)S(1)} all-to-all(f32[32,32,128]{2,1,0:T(8,128)S(1)} %bitcast.38), channel_id=1, replica_groups=mesh['zh'=2,'y'=8,'zl'=6,'x'=4,'c'=2] {'y','x'}, dimensions={0} | all-to-all | bytes 1048576 | tf_op jit(solution)/shard_map/all_to_all | solution.py:117
  155.1 0.6 reshape.99
  (2 shorter events, 0.1 us)
Async XLA Ops:
  6.5 22.5 %copy-start = (s32[2,3072]{1,0:T(2,128)S(1)}, s32[2,3072]{1,0:T(2,128)}, u32[]{:S(2)}) copy-start(s32[2,3072]{1,0:T(2,128)} %param.11) | copy-start | bytes 73732
  6.5 22.6 %copy-start.2 = (s32[48]{0:T(128)S(1)}, s32[48]{0:T(128)}, u32[]{:S(2)}) copy-start(s32[48]{0:T(128)} %slab_ref.1) | copy-start | bytes 580
  6.5 22.6 %copy-start.3 = (s32[16,256]{1,0:T(8,128)S(1)}, s32[16,256]{1,0:T(8,128)}, u32[]{:S(2)}) copy-start(s32[16,256]{1,0:T(8,128)} %param.8) | copy-start | bytes 49156
  6.5 22.9 %copy-start.1 = (bf16[4,48,4096]{2,1,0:T(8,128)(2,1)S(1)}, bf16[4,48,4096]{2,1,0:T(8,128)(2,1)}, u32[]{:S(2)}) copy-start(bf16[4,48,4096]{2,1,0:T(8,128)(2,1)} %param.6) | copy-start | bytes 4718596
  6.5 114.2 %all-gather.2.cloned.1.call-start = ((), (), s32[]{:S(2)}) async-start(), calls=%async_computation.3 | async-start | bytes 6815744 | tf_op jit(solution)/shard_map/all_gather | solution.py:82
  125.2 4.1 %collective-permute-start = (f32[1024,128]{1,0:T(8,128)S(1)}, f32[1024,128]{1,0:T(8,128)S(1)}, u32[]{:S(2)}, u32[]{:S(2)}) collective-permute-start(f32[1024,128]{1,0:T(8,128)S(1)} %get-tuple-element.10), channel_id=1, source_target_pairs={{0,1},{1,0},{2,3},{3,2},{4,5},{5,4},{6,7},{7,6},{8,9},{9,8},{10,11... | collective-permute-start | bytes 1572872 | tf_op jit(solution)/shard_map/ppermute | solution.py:115
Sparse Core Ops, SparseCore 0:
  29.1 91.5 all-gather.1

commit v4 on v3

--- a/solution.py
+++ b/solution.py
@@ -12,6 +12,8 @@
 NOCC = 200
 OT = (NOCC + TILE - 1) // TILE
 ZH, Y, ZL, X, CORE = 2, 8, 6, 4, 2
+RING = ZH * ZL
+LANES = 128
 ALL = ("zh", "y", "zl", "x", "c")
 
 
@@ -27,13 +29,23 @@
         out[y] = b_ref[:, y * width : (y + 1) * width] * keep
 
 
-def ladder(core_ref, a_ref, b_ref, mine_ref, other_ref, held, landed):
-    core = core_ref[0]
-    width = b_ref.shape[3]
+def ladder(where_ref, a_ref, b_ref, *rest):
+    near = rest[:RING]
+    mine_ref, other_ref, held, landed, near_landed = rest[RING:]
+    core, place = where_ref[0], where_ref[1]
+    width = b_ref.shape[3] + LANES
+    for e, ref in enumerate(near):
+        spot = (place + e) % RING
+        column = pl.multiple_of((spot % ZL) * width + (width - LANES), LANES)
+        pltpu.make_async_copy(
+            ref, held.at[spot // ZL, :, pl.ds(column, LANES)], near_landed.at[e]
+        ).start()
     copies = [
         [
             pltpu.make_async_copy(
-                b_ref.at[zh, zl], held.at[zh, :, pl.ds(zl * width, width)], landed.at[zh, zl]
+                b_ref.at[zh, zl],
+                held.at[zh, :, pl.ds(zl * width, width - LANES)],
+                landed.at[zh, zl],
             )
             for zl in range(ZL)
         ]
@@ -42,6 +54,8 @@
     for group in copies:
         for copy in group:
             copy.start()
+    for e, ref in enumerate(near):
+        pltpu.make_async_copy(ref, held.at[0, :, pl.ds(0, LANES)], near_landed.at[e]).wait()
     per = a_ref.shape[1]
     chips = Y * X
     stride = mine_ref.shape[0] // chips
@@ -79,8 +93,16 @@
         out_specs=pl.BlockSpec(memory_space=pltpu.VMEM),
     )(jnp.stack([block, owner]).astype(jnp.int32), slab_ids, int_pattern, integrals.reshape(rows, depth))
     moved = lax.all_to_all(ready, "y", 0, 0, tiled=True)
-    gathered = lax.all_gather(moved.reshape(Y * rows, width), ("zh", "zl"), axis=0, tiled=True)
-    gathered = gathered.reshape(ZH, ZL, Y * rows, width)
+    moved = moved.reshape(Y * rows, width)
+    gathered = lax.all_gather(moved[:, : width - LANES], ("zh", "zl"), axis=0, tiled=True)
+    gathered = gathered.reshape(ZH, ZL, Y * rows, width - LANES)
+    up = [(z, (z + 1) % RING) for z in range(RING)]
+    down = [(z, (z - 1) % RING) for z in range(RING)]
+    near = {0: moved[:, width - LANES :]}
+    for step in range(RING // 2):
+        near[RING - 1 - step] = lax.ppermute(near[(RING - step) % RING], ("zh", "zl"), up)
+        if step + 1 < RING // 2:
+            near[step + 1] = lax.ppermute(near[step], ("zh", "zl"), down)
 
     window = lax.dynamic_slice_in_dim(pair_window, (block * (ZL * X * CORE) + owner) * pairs, pairs, 1)
     occ_tile = window[0] // TILE * OT + window[1] // TILE
@@ -101,17 +123,25 @@
     mine, other = pl.pallas_call(
         ladder,
         out_shape=[jax.ShapeDtypeStruct((out_rows, 128), jnp.float32)] * 2,
-        in_specs=[smem, pl.BlockSpec(memory_space=pltpu.VMEM), pl.BlockSpec(memory_space=pltpu.HBM)],
+        in_specs=[
+            smem,
+            pl.BlockSpec(memory_space=pltpu.VMEM),
+            pl.BlockSpec(memory_space=pltpu.HBM),
+        ]
+        + [pl.BlockSpec(memory_space=pl.ANY)] * RING,
         out_specs=[pl.BlockSpec(memory_space=pltpu.VMEM)] * 2,
         scratch_shapes=[
             pltpu.VMEM((ZH, Y * rows, ZL * width), jnp.bfloat16),
             pltpu.SemaphoreType.DMA((ZH, ZL)),
+            pltpu.SemaphoreType.DMA((RING,)),
         ],
         compiler_params=pltpu.CompilerParams(vmem_limit_bytes=48 * 1024 * 1024),
         cost_estimate=pl.CostEstimate(
             flops=4 * pairs * Y * X * cols * ZL * width, bytes_accessed=8 * 1024 * 1024, transcendentals=0
         ),
-    )(c.reshape(1).astype(jnp.int32), amps, gathered)
+    )(
+        jnp.stack([c, zh * ZL + zl]).astype(jnp.int32), amps, gathered, *[near[e] for e in range(RING)]
+    )
     got = lax.ppermute(other, "c", [(0, 1), (1, 0)])
     summed = (mine + got).reshape(Y * X, pairs * lines, 128)
     sums = lax.all_to_all(summed, ("y", "x"), 0, 0, tiled=True)

time: 163 us -> 167 us (1.025)
  starting transfers between devices: 2.61 us -> 57.7 us
  blocking collectives: 96 us -> 45.5 us
  waiting for transfers between devices: 34.4 us -> 26.4 us
  local copies, waits for them, and re-layouts: 8.56 us -> 13.7 us
    all_to_all x1 -> x0, blocking collectives: 50.4 us -> none  [per_device(): swapped = lax.all_to_all(masked, ('y', 'x', 'c'), 0, 0, tiled=True)]
    ppermute x0 -> x11, starting transfers between devices: none -> 43.7 us  [the longest x5 30.5 us: per_device(): near[step + 1] = lax.ppermute(near[step], ('zh', 'zl'), down)]
    all_gather x1, waiting for transfers between devices: 32.8 us -> 4.3 us  [per_device(): lax.all_gather(moved[:, :width - LANES], ('zh', 'zl'), axis=0, tiled=True)]
    ppermute x0 -> x11, waiting for transfers between devices: none -> 20.6 us  [the longest x6 20.6 us: per_device(): lax.ppermute(near[(RING - step) % RING], ('zh', 'zl'), up)]
    all_to_all x0 -> x1, starting transfers between devices: none -> 11.4 us  [per_device(): swapped = lax.all_to_all(masked, ('y', 'x', 'c'), 0, 0, tiled=True)]
    reshape x1, local copies, waits for them, and re-layouts: 0.65 us -> 2.52 us  [per_device(): swapped.reshape(Y * X, CORE, pairs, ZL, width).transpose(1, 2, 0, 3, 4)]
  transfers between devices with their start and end apart: 2 -> 14, of which waited for: 2 -> 7; matrix products, arithmetic and copies ran while one was open for 5% -> 8% of each run, Pallas kernels for 0% -> 0%
where the time goes in v4:
time: 167 us; the launch traced here: 166 us
  starting transfers between devices  57.7 us (35%)
  blocking collectives  45.5 us (27%)
  waiting for transfers between devices  26.4 us (16%)
  local copies, waits for them, and re-layouts  13.7 us (8%)
  between operations  13.6 us (8%)
  Pallas kernels  7.49 us (4%)
    ppermute x5, starting transfers between devices, per_device(): near[step + 1] = lax.ppermute(near[step], ('zh', 'zl'), down)  30.5 us
    all_to_all x1, blocking collectives, per_device(): sums = lax.all_to_all(summed, ('y', 'x'), 0, 0, tiled=True)  25.6 us
    ppermute x6, waiting for transfers between devices, per_device(): lax.ppermute(near[(RING - step) % RING], ('zh', 'zl'), up)  20.6 us
    all_to_all x1, blocking collectives, per_device(): moved = lax.all_to_all(ready, 'y', 0, 0, tiled=True)  19.9 us
    ppermute x6, starting transfers between devices, per_device(): lax.ppermute(near[(RING - step) % RING], ('zh', 'zl'), up)  13.2 us
    all_to_all x1, starting transfers between devices, per_device(): swapped = lax.all_to_all(masked, ('y', 'x', 'c'), 0, 0, tiled=True)  11.4 us
    pallas_call x1, Pallas kernels, per_device(): pl.pallas_call(ladder, out_shape=[jax.ShapeDtypeStruct((out_rows, 128), j...  5.46 us
    all_gather x1, waiting for transfers between devices, per_device(): lax.all_gather(moved[:, :width - LANES], ('zh', 'zl'), axis=0, tiled=True)  4.3 us
  transfers between devices with their start and end apart: 14, of which 7 were waited for; matrix products, arithmetic and copies ran while one was open for 8% of the time, Pallas kernels for 0%

profile of v4, /device:TPU:1, one launch (start us, length us, event | category | flops | bytes accessed | tf_op | source)
XLA Modules:
  0.0 165.7 jit_solution(10089361602636452899)
XLA Ops:
  6.5 0.6 pad_add_fusion.1.where_ref
  7.2 2.0 %shard_map.64 = bf16[8,64,512]{2,1,0:T(8,128)(2,1)} custom-call(s32[2]{0:T(128)} %pad_add_fusion.1.where_ref, s32[48]{0:T(128)} %slab_ref.1, s32[16,256]{1,0:T(8,128)} %pattern_ref.1, bf16[64,4096]{1,0:T(8,128)(2,1)} %bitcast.42), custom_call_target="tpu_custom_call" | custom-call | tf_op jit(solution)/shard_map/pallas_call | solution.py:89
  9.2 19.9 %all_to_all.15 = bf16[8,64,512]{2,1,0:T(8,128)(2,1)S(1)} all-to-all(bf16[8,64,512]{2,1,0:T(8,128)(2,1)} %shard_map.64), channel_id=1, replica_groups=mesh['zh'=2,'y'=8,'zl'=6,'x'=4,'c'=2] {'y'}, dimensions={0} | all-to-all | bytes 1048576 | tf_op jit(solution)/shard_map/all_to_all | solution.py:95
  29.1 0.8 slice.16
  30.5 2.1 %copy.11 = bf16[64,24,512]{2,1,0:T(8,128)(2,1)} copy(bf16[64,24,512]{2,0,1:T(8,128)(2,1)S(1)} %bitcast.36) | data formatting | bytes 3145728 | tf_op jit(solution)/shard_map/optimization_barrier | solution.py:114
  32.6 11.4 %all-to-all-start.1 = ((bf16[64,24,512]{2,1,0:T(8,128)(2,1)}), bf16[64,24,512]{2,1,0:T(8,128)(2,1)S(1)}, u32[]{:S(2)}, u32[]{:S(2)}) async-start(bf16[64,24,512]{2,1,0:T(8,128)(2,1)} %copy.11), calls=%async_computation.1 | async-start | bytes 3145728 | tf_op jit(solution)/shard_map/all_to_all | solution.py:115
  44.0 3.7 %collective-permute-start.5 = (bf16[512,128]{1,0:T(8,128)(2,1)S(1)}, bf16[512,128]{1,0:T(8,128)(2,1)S(1)}, u32[]{:S(2)}, u32[]{:S(2)}) collective-permute-start(bf16[512,128]{1,0:T(8,128)(2,1)S(1)} %slice.17.rest_0_), channel_id=1, source_target_pairs={{0,8},{8,16},{16,24},{24,32},{32,40},{40,384},{384,392},{392,400},... | collective-permute-start | bytes 393224 | tf_op jit(solution)/shard_map/ppermute | solution.py:103
  47.7 12.2 %collective-permute-start = (bf16[512,128]{1,0:T(8,128)(2,1)S(1)}, bf16[512,128]{1,0:T(8,128)(2,1)S(1)}, u32[]{:S(2)}, u32[]{:S(2)}) collective-permute-start(bf16[512,128]{1,0:T(8,128)(2,1)S(1)} %slice.17.rest_0_), channel_id=1, source_target_pairs={{0,424},{8,0},{16,8},{24,16},{32,24},{40,32},{384,40},{392,384},{4... | collective-permute-start | bytes 393224 | tf_op jit(solution)/shard_map/ppermute | solution.py:105
  59.9 4.8 %collective-permute-done.5.rest_11_ = bf16[512,128]{1,0:T(8,128)(2,1)S(1)} collective-permute-done((bf16[512,128]{1,0:T(8,128)(2,1)S(1)}, bf16[512,128]{1,0:T(8,128)(2,1)S(1)}, u32[]{:S(2)}, u32[]{:S(2)}) %collective-permute-start.5) | collective-permute-done | bytes 131104 | tf_op jit(solution)/shard_map/ppermute | solution.py:103
  64.7 1.9 %collective-permute-start.6 = (bf16[512,128]{1,0:T(8,128)(2,1)S(1)}, bf16[512,128]{1,0:T(8,128)(2,1)S(1)}, u32[]{:S(2)}, u32[]{:S(2)}) collective-permute-start(bf16[512,128]{1,0:T(8,128)(2,1)S(1)} %collective-permute-done.5.rest_11_), channel_id=1, source_target_pairs={{0,8},{8,16},{16,24},{24,32},{32,40},{40,384},{384,392},{392,400},... | collective-permute-start | bytes 393224 | tf_op jit(solution)/shard_map/ppermute | solution.py:103
  66.6 4.6 %collective-permute-start.1 = (bf16[512,128]{1,0:T(8,128)(2,1)S(1)}, bf16[512,128]{1,0:T(8,128)(2,1)S(1)}, u32[]{:S(2)}, u32[]{:S(2)}) collective-permute-start(bf16[512,128]{1,0:T(8,128)(2,1)S(1)} %collective-permute-done.rest_1_), channel_id=1, source_target_pairs={{0,424},{8,0},{16,8},{24,16},{32,24},{40,32},{384,40},{392,384},{4... | collective-permute-start | bytes 393224 | tf_op jit(solution)/shard_map/ppermute | solution.py:105
  71.2 4.5 %collective-permute-done.6.rest_10_ = bf16[512,128]{1,0:T(8,128)(2,1)S(1)} collective-permute-done((bf16[512,128]{1,0:T(8,128)(2,1)S(1)}, bf16[512,128]{1,0:T(8,128)(2,1)S(1)}, u32[]{:S(2)}, u32[]{:S(2)}) %collective-permute-start.6) | collective-permute-done | bytes 131104 | tf_op jit(solution)/shard_map/ppermute | solution.py:103
  75.7 1.9 %collective-permute-start.7 = (bf16[512,128]{1,0:T(8,128)(2,1)S(1)}, bf16[512,128]{1,0:T(8,128)(2,1)S(1)}, u32[]{:S(2)}, u32[]{:S(2)}) collective-permute-start(bf16[512,128]{1,0:T(8,128)(2,1)S(1)} %collective-permute-done.6.rest_10_), channel_id=1, source_target_pairs={{0,8},{8,16},{16,24},{24,32},{32,40},{40,384},{384,392},{392,400},... | collective-permute-start | bytes 393224 | tf_op jit(solution)/shard_map/ppermute | solution.py:103
  77.6 4.6 %collective-permute-start.2 = (bf16[512,128]{1,0:T(8,128)(2,1)S(1)}, bf16[512,128]{1,0:T(8,128)(2,1)S(1)}, u32[]{:S(2)}, u32[]{:S(2)}) collective-permute-start(bf16[512,128]{1,0:T(8,128)(2,1)S(1)} %collective-permute-done.1.rest_2_), channel_id=1, source_target_pairs={{0,424},{8,0},{16,8},{24,16},{32,24},{40,32},{384,40},{392,384},{4... | collective-permute-start | bytes 393224 | tf_op jit(solution)/shard_map/ppermute | solution.py:105
  82.2 4.1 %collective-permute-done.7.rest_9_ = bf16[512,128]{1,0:T(8,128)(2,1)S(1)} collective-permute-done((bf16[512,128]{1,0:T(8,128)(2,1)S(1)}, bf16[512,128]{1,0:T(8,128)(2,1)S(1)}, u32[]{:S(2)}, u32[]{:S(2)}) %collective-permute-start.7) | collective-permute-done | bytes 131104 | tf_op jit(solution)/shard_map/ppermute | solution.py:103
  86.2 1.9 %collective-permute-start.8 = (bf16[512,128]{1,0:T(8,128)(2,1)S(1)}, bf16[512,128]{1,0:T(8,128)(2,1)S(1)}, u32[]{:S(2)}, u32[]{:S(2)}) collective-permute-start(bf16[512,128]{1,0:T(8,128)(2,1)S(1)} %collective-permute-done.7.rest_9_), channel_id=1, source_target_pairs={{0,8},{8,16},{16,24},{24,32},{32,40},{40,384},{384,392},{392,400},... | collective-permute-start | bytes 393224 | tf_op jit(solution)/shard_map/ppermute | solution.py:103
  88.2 4.6 %collective-permute-start.3 = (bf16[512,128]{1,0:T(8,128)(2,1)S(1)}, bf16[512,128]{1,0:T(8,128)(2,1)S(1)}, u32[]{:S(2)}, u32[]{:S(2)}) collective-permute-start(bf16[512,128]{1,0:T(8,128)(2,1)S(1)} %collective-permute-done.2.rest_3_), channel_id=1, source_target_pairs={{0,424},{8,0},{16,8},{24,16},{32,24},{40,32},{384,40},{392,384},{4... | collective-permute-start | bytes 393224 | tf_op jit(solution)/shard_map/ppermute | solution.py:105
  92.7 4.0 %collective-permute-done.8.rest_8_ = bf16[512,128]{1,0:T(8,128)(2,1)S(1)} collective-permute-done((bf16[512,128]{1,0:T(8,128)(2,1)S(1)}, bf16[512,128]{1,0:T(8,128)(2,1)S(1)}, u32[]{:S(2)}, u32[]{:S(2)}) %collective-permute-start.8) | collective-permute-done | bytes 131104 | tf_op jit(solution)/shard_map/ppermute | solution.py:103
  96.7 1.9 %collective-permute-start.9 = (bf16[512,128]{1,0:T(8,128)(2,1)S(1)}, bf16[512,128]{1,0:T(8,128)(2,1)S(1)}, u32[]{:S(2)}, u32[]{:S(2)}) collective-permute-start(bf16[512,128]{1,0:T(8,128)(2,1)S(1)} %collective-permute-done.8.rest_8_), channel_id=1, source_target_pairs={{0,8},{8,16},{16,24},{24,32},{32,40},{40,384},{384,392},{392,400},... | collective-permute-start | bytes 393224 | tf_op jit(solution)/shard_map/ppermute | solution.py:103
  98.6 4.6 %collective-permute-start.4 = (bf16[512,128]{1,0:T(8,128)(2,1)S(1)}, bf16[512,128]{1,0:T(8,128)(2,1)S(1)}, u32[]{:S(2)}, u32[]{:S(2)}) collective-permute-start(bf16[512,128]{1,0:T(8,128)(2,1)S(1)} %collective-permute-done.3.rest_4_), channel_id=1, source_target_pairs={{0,424},{8,0},{16,8},{24,16},{32,24},{40,32},{384,40},{392,384},{4... | collective-permute-start | bytes 393224 | tf_op jit(solution)/shard_map/ppermute | solution.py:105
  103.2 3.3 %collective-permute-done.9.rest_7_ = bf16[512,128]{1,0:T(8,128)(2,1)S(1)} collective-permute-done((bf16[512,128]{1,0:T(8,128)(2,1)S(1)}, bf16[512,128]{1,0:T(8,128)(2,1)S(1)}, u32[]{:S(2)}, u32[]{:S(2)}) %collective-permute-start.9) | collective-permute-done | bytes 131104 | tf_op jit(solution)/shard_map/ppermute | solution.py:103
  106.5 1.9 %collective-permute-start.10 = (bf16[512,128]{1,0:T(8,128)(2,1)S(1)}, bf16[512,128]{1,0:T(8,128)(2,1)S(1)}, u32[]{:S(2)}, u32[]{:S(2)}) collective-permute-start(bf16[512,128]{1,0:T(8,128)(2,1)S(1)} %collective-permute-done.9.rest_7_), channel_id=1, source_target_pairs={{0,8},{8,16},{16,24},{24,32},{32,40},{40,384},{384,392},{392,400},... | collective-permute-start | bytes 393224 | tf_op jit(solution)/shard_map/ppermute | solution.py:103
  108.5 1.7 %copy.12 = bf16[64,24,512]{2,0,1:T(8,128)(2,1)} copy(bf16[64,24,512]{2,1,0:T(8,128)(2,1)S(1)} %all-to-all-done.1) | data formatting | bytes 3145728 | tf_op jit(solution)/shard_map/all_to_all | solution.py:115
  110.2 2.5 %reshape.91 = bf16[32,2,4,6,512]{4,1,0,3,2:T(2,128)(2,1)S(1)} reshape(bf16[64,24,512]{2,0,1:T(8,128)(2,1)} %copy.12) | data formatting | bytes 3145728 | tf_op jit(solution)/shard_map/reshape | solution.py:116
  112.8 2.3 %copy.13 = bf16[2,4,32,6,512]{4,3,2,1,0:T(8,128)(2,1)} copy(bf16[2,4,32,6,512]{4,0,2,3,1:T(2,128)(2,1)S(1)} %bitcast.37) | data formatting | bytes 3145728 | tf_op jit(solution)/shard_map/transpose | solution.py:116
  115.0 3.6 %reshape.92.a_ref = bf16[2,128,3072]{2,1,0:T(8,128)(2,1)S(1)} reshape(bf16[2,4,32,6,512]{4,3,2,1,0:T(8,128)(2,1)} %copy.13) | data formatting | bytes 3145728 | tf_op jit(solution)/shard_map/reshape | solution.py:117
  118.6 4.3 %all-gather.2.cloned.1.call-done = bf16[6144,384]{1,0:T(8,128)(2,1)} async-done(((bf16[512,384]{1,0:T(8,128)(2,1)}), bf16[6144,384]{1,0:T(8,128)(2,1)}) %all-gather.2.cloned.1.call-update) | async-done | bytes 4718608 | tf_op jit(solution)/shard_map/all_gather | solution.py:97
  122.9 5.5 %shard_map.65 = (f32[1024,128]{1,0:T(8,128)S(1)}, f32[1024,128]{1,0:T(8,128)S(1)}) custom-call(s32[2]{0:T(128)S(1)} %pad_add_fusion.where_ref, bf16[2,128,3072]{2,1,0:T(8,128)(2,1)S(1)} %reshape.92.a_ref, bf16[2,6,512,384]{3,2,1,0:T(8,128)(2,1)} %bitcast.38, bf16[512,128]{1,0:T(8,128)(2,1)S(1)} %slice.17.rest_0_, ...), custom_call_target="tpu_custom_call" | custom-call | flops 1610612736 | bytes 8388608 | tf_op jit(solution)/shard_map/pallas_call | solution.py:123
  128.4 2.6 %collective-permute-start.11 = (f32[1024,128]{1,0:T(8,128)S(1)}, f32[1024,128]{1,0:T(8,128)S(1)}, u32[]{:S(2)}, u32[]{:S(2)}) collective-permute-start(f32[1024,128]{1,0:T(8,128)S(1)} %get-tuple-element.10), channel_id=1, source_target_pairs={{0,1},{1,0},{2,3},{3,2},{4,5},{5,4},{6,7},{7,6},{8,9},{9,8},{10,11... | collective-permute-start | bytes 1572872 | tf_op jit(solution)/shard_map/ppermute | solution.py:145
  131.0 1.5 collective-permute-done.11
  132.6 25.6 %all_to_all.16 = f32[32,32,128]{2,1,0:T(8,128)S(1)} all-to-all(f32[32,32,128]{2,1,0:T(8,128)S(1)} %bitcast.39), channel_id=1, replica_groups=mesh['zh'=2,'y'=8,'zl'=6,'x'=4,'c'=2] {'y','x'}, dimensions={0} | all-to-all | bytes 1048576 | tf_op jit(solution)/shard_map/all_to_all | solution.py:147
  158.3 0.6 reshape.95
  (25 shorter events, 0.8 us)
Async XLA Ops:
  6.5 23.4 %copy-start = (s32[2,3072]{1,0:T(2,128)S(1)}, s32[2,3072]{1,0:T(2,128)}, u32[]{:S(2)}) copy-start(s32[2,3072]{1,0:T(2,128)} %param.11) | copy-start | bytes 73732
  6.5 116.4 %all-gather.2.cloned.1.call-start = ((), (), s32[]{:S(2)}) async-start(), calls=%async_computation.3 | async-start | bytes 5111808 | tf_op jit(solution)/shard_map/all_gather | solution.py:97
  7.1 22.9 %copy-start.2 = (s32[48]{0:T(128)S(1)}, s32[48]{0:T(128)}, u32[]{:S(2)}) copy-start(s32[48]{0:T(128)} %slab_ref.1) | copy-start | bytes 580
  7.1 22.9 %copy-start.3 = (s32[16,256]{1,0:T(8,128)S(1)}, s32[16,256]{1,0:T(8,128)}, u32[]{:S(2)}) copy-start(s32[16,256]{1,0:T(8,128)} %param.8) | copy-start | bytes 49156
  7.2 23.2 %copy-start.1 = (bf16[4,48,4096]{2,1,0:T(8,128)(2,1)S(1)}, bf16[4,48,4096]{2,1,0:T(8,128)(2,1)}, u32[]{:S(2)}) copy-start(bf16[4,48,4096]{2,1,0:T(8,128)(2,1)} %param.6) | copy-start | bytes 4718596
  32.6 76.0 %all-to-all-start.1 = ((bf16[64,24,512]{2,1,0:T(8,128)(2,1)}), bf16[64,24,512]{2,1,0:T(8,128)(2,1)S(1)}, u32[]{:S(2)}, u32[]{:S(2)}) async-start(bf16[64,24,512]{2,1,0:T(8,128)(2,1)} %copy.11), calls=%async_computation.1 | async-start | bytes 3145728 | tf_op jit(solution)/shard_map/all_to_all | solution.py:115
  44.0 20.7 %collective-permute-start.5 = (bf16[512,128]{1,0:T(8,128)(2,1)S(1)}, bf16[512,128]{1,0:T(8,128)(2,1)S(1)}, u32[]{:S(2)}, u32[]{:S(2)}) collective-permute-start(bf16[512,128]{1,0:T(8,128)(2,1)S(1)} %slice.17.rest_0_), channel_id=1, source_target_pairs={{0,8},{8,16},{16,24},{24,32},{32,40},{40,384},{384,392},{392,400},... | collective-permute-start | bytes 393224 | tf_op jit(solution)/shard_map/ppermute | solution.py:103
  47.7 19.0 %collective-permute-start = (bf16[512,128]{1,0:T(8,128)(2,1)S(1)}, bf16[512,128]{1,0:T(8,128)(2,1)S(1)}, u32[]{:S(2)}, u32[]{:S(2)}) collective-permute-start(bf16[512,128]{1,0:T(8,128)(2,1)S(1)} %slice.17.rest_0_), channel_id=1, source_target_pairs={{0,424},{8,0},{16,8},{24,16},{32,24},{40,32},{384,40},{392,384},{4... | collective-permute-start | bytes 393224 | tf_op jit(solution)/shard_map/ppermute | solution.py:105
  64.7 11.0 %collective-permute-start.6 = (bf16[512,128]{1,0:T(8,128)(2,1)S(1)}, bf16[512,128]{1,0:T(8,128)(2,1)S(1)}, u32[]{:S(2)}, u32[]{:S(2)}) collective-permute-start(bf16[512,128]{1,0:T(8,128)(2,1)S(1)} %collective-permute-done.5.rest_11_), channel_id=1, source_target_pairs={{0,8},{8,16},{16,24},{24,32},{32,40},{40,384},{384,392},{392,400},... | collective-permute-start | bytes 393224 | tf_op jit(solution)/shard_map/ppermute | solution.py:103
  66.6 11.0 %collective-permute-start.1 = (bf16[512,128]{1,0:T(8,128)(2,1)S(1)}, bf16[512,128]{1,0:T(8,128)(2,1)S(1)}, u32[]{:S(2)}, u32[]{:S(2)}) collective-permute-start(bf16[512,128]{1,0:T(8,128)(2,1)S(1)} %collective-permute-done.rest_1_), channel_id=1, source_target_pairs={{0,424},{8,0},{16,8},{24,16},{32,24},{40,32},{384,40},{392,384},{4... | collective-permute-start | bytes 393224 | tf_op jit(solution)/shard_map/ppermute | solution.py:105
  75.7 10.6 %collective-permute-start.7 = (bf16[512,128]{1,0:T(8,128)(2,1)S(1)}, bf16[512,128]{1,0:T(8,128)(2,1)S(1)}, u32[]{:S(2)}, u32[]{:S(2)}) collective-permute-start(bf16[512,128]{1,0:T(8,128)(2,1)S(1)} %collective-permute-done.6.rest_10_), channel_id=1, source_target_pairs={{0,8},{8,16},{16,24},{24,32},{32,40},{40,384},{384,392},{392,400},... | collective-permute-start | bytes 393224 | tf_op jit(solution)/shard_map/ppermute | solution.py:103
  77.6 10.6 %collective-permute-start.2 = (bf16[512,128]{1,0:T(8,128)(2,1)S(1)}, bf16[512,128]{1,0:T(8,128)(2,1)S(1)}, u32[]{:S(2)}, u32[]{:S(2)}) collective-permute-start(bf16[512,128]{1,0:T(8,128)(2,1)S(1)} %collective-permute-done.1.rest_2_), channel_id=1, source_target_pairs={{0,424},{8,0},{16,8},{24,16},{32,24},{40,32},{384,40},{392,384},{4... | collective-permute-start | bytes 393224 | tf_op jit(solution)/shard_map/ppermute | solution.py:105
  86.2 10.5 %collective-permute-start.8 = (bf16[512,128]{1,0:T(8,128)(2,1)S(1)}, bf16[512,128]{1,0:T(8,128)(2,1)S(1)}, u32[]{:S(2)}, u32[]{:S(2)}) collective-permute-start(bf16[512,128]{1,0:T(8,128)(2,1)S(1)} %collective-permute-done.7.rest_9_), channel_id=1, source_target_pairs={{0,8},{8,16},{16,24},{24,32},{32,40},{40,384},{384,392},{392,400},... | collective-permute-start | bytes 393224 | tf_op jit(solution)/shard_map/ppermute | solution.py:103
  88.2 10.5 %collective-permute-start.3 = (bf16[512,128]{1,0:T(8,128)(2,1)S(1)}, bf16[512,128]{1,0:T(8,128)(2,1)S(1)}, u32[]{:S(2)}, u32[]{:S(2)}) collective-permute-start(bf16[512,128]{1,0:T(8,128)(2,1)S(1)} %collective-permute-done.2.rest_3_), channel_id=1, source_target_pairs={{0,424},{8,0},{16,8},{24,16},{32,24},{40,32},{384,40},{392,384},{4... | collective-permute-start | bytes 393224 | tf_op jit(solution)/shard_map/ppermute | solution.py:105
  96.7 9.8 %collective-permute-start.9 = (bf16[512,128]{1,0:T(8,128)(2,1)S(1)}, bf16[512,128]{1,0:T(8,128)(2,1)S(1)}, u32[]{:S(2)}, u32[]{:S(2)}) collective-permute-start(bf16[512,128]{1,0:T(8,128)(2,1)S(1)} %collective-permute-done.8.rest_8_), channel_id=1, source_target_pairs={{0,8},{8,16},{16,24},{24,32},{32,40},{40,384},{384,392},{392,400},... | collective-permute-start | bytes 393224 | tf_op jit(solution)/shard_map/ppermute | solution.py:103
  98.6 20.0 %collective-permute-start.4 = (bf16[512,128]{1,0:T(8,128)(2,1)S(1)}, bf16[512,128]{1,0:T(8,128)(2,1)S(1)}, u32[]{:S(2)}, u32[]{:S(2)}) collective-permute-start(bf16[512,128]{1,0:T(8,128)(2,1)S(1)} %collective-permute-done.3.rest_4_), channel_id=1, source_target_pairs={{0,424},{8,0},{16,8},{24,16},{32,24},{40,32},{384,40},{392,384},{4... | collective-permute-start | bytes 393224 | tf_op jit(solution)/shard_map/ppermute | solution.py:105
  106.5 12.1 %collective-permute-start.10 = (bf16[512,128]{1,0:T(8,128)(2,1)S(1)}, bf16[512,128]{1,0:T(8,128)(2,1)S(1)}, u32[]{:S(2)}, u32[]{:S(2)}) collective-permute-start(bf16[512,128]{1,0:T(8,128)(2,1)S(1)} %collective-permute-done.9.rest_7_), channel_id=1, source_target_pairs={{0,8},{8,16},{16,24},{24,32},{32,40},{40,384},{384,392},{392,400},... | collective-permute-start | bytes 393224 | tf_op jit(solution)/shard_map/ppermute | solution.py:103
  128.4 4.1 %collective-permute-start.11 = (f32[1024,128]{1,0:T(8,128)S(1)}, f32[1024,128]{1,0:T(8,128)S(1)}, u32[]{:S(2)}, u32[]{:S(2)}) collective-permute-start(f32[1024,128]{1,0:T(8,128)S(1)} %get-tuple-element.10), channel_id=1, source_target_pairs={{0,1},{1,0},{2,3},{3,2},{4,5},{5,4},{6,7},{7,6},{8,9},{9,8},{10,11... | collective-permute-start | bytes 1572872 | tf_op jit(solution)/shard_map/ppermute | solution.py:145
Sparse Core Ops, SparseCore 0:
  30.0 92.8 all-gather.1

commit v5 on v3

--- a/solution.py
+++ b/solution.py
@@ -27,14 +27,18 @@
         out[y] = b_ref[:, y * width : (y + 1) * width] * keep
 
 
-def ladder(core_ref, a_ref, b_ref, mine_ref, other_ref, held, landed):
+def ladder(core_ref, a_ref, b_ref, last_ref, mine_ref, other_ref, held, landed):
     core = core_ref[0]
     width = b_ref.shape[3]
+    rows = (0, b_ref.shape[2], b_ref.shape[2] + last_ref.shape[2])
     copies = [
         [
             pltpu.make_async_copy(
-                b_ref.at[zh, zl], held.at[zh, :, pl.ds(zl * width, width)], landed.at[zh, zl]
+                ref.at[zh, zl],
+                held.at[zh, pl.ds(rows[n], rows[n + 1] - rows[n]), pl.ds(zl * width, width)],
+                landed.at[n, zh, zl],
             )
+            for n, ref in enumerate((b_ref, last_ref))
             for zl in range(ZL)
         ]
         for zh in range(ZH)
@@ -79,8 +83,9 @@
         out_specs=pl.BlockSpec(memory_space=pltpu.VMEM),
     )(jnp.stack([block, owner]).astype(jnp.int32), slab_ids, int_pattern, integrals.reshape(rows, depth))
     moved = lax.all_to_all(ready, "y", 0, 0, tiled=True)
-    gathered = lax.all_gather(moved.reshape(Y * rows, width), ("zh", "zl"), axis=0, tiled=True)
-    gathered = gathered.reshape(ZH, ZL, Y * rows, width)
+    most = moved[: Y - 1].reshape((Y - 1) * rows, width)
+    gathered = lax.all_gather(most, ("zh", "zl"), axis=0, tiled=True)
+    gathered = gathered.reshape(ZH, ZL, (Y - 1) * rows, width)
 
     window = lax.dynamic_slice_in_dim(pair_window, (block * (ZL * X * CORE) + owner) * pairs, pairs, 1)
     occ_tile = window[0] // TILE * OT + window[1] // TILE
@@ -89,8 +94,9 @@
     masked = amplitudes * mask[:, :, None]
     masked = masked.reshape(pairs, ZL, X * CORE, Y, width).transpose(3, 2, 0, 1, 4)
     masked = masked.reshape(Y * X * CORE, pairs * ZL, width)
-    masked, _ = lax.optimization_barrier((masked, moved))
+    masked, last = lax.optimization_barrier((masked, moved[Y - 1]))
     swapped = lax.all_to_all(masked, ("y", "x", "c"), 0, 0, tiled=True)
+    last = lax.all_gather(last, ("zh", "zl"), axis=0, tiled=True).reshape(ZH, ZL, rows, width)
     amps = swapped.reshape(Y * X, CORE, pairs, ZL, width).transpose(1, 2, 0, 3, 4)
     amps = amps.reshape(CORE, pairs * Y * X, ZL * width)
 
@@ -101,17 +107,22 @@
     mine, other = pl.pallas_call(
         ladder,
         out_shape=[jax.ShapeDtypeStruct((out_rows, 128), jnp.float32)] * 2,
-        in_specs=[smem, pl.BlockSpec(memory_space=pltpu.VMEM), pl.BlockSpec(memory_space=pltpu.HBM)],
+        in_specs=[
+            smem,
+            pl.BlockSpec(memory_space=pltpu.VMEM),
+            pl.BlockSpec(memory_space=pltpu.HBM),
+            pl.BlockSpec(memory_space=pl.ANY),
+        ],
         out_specs=[pl.BlockSpec(memory_space=pltpu.VMEM)] * 2,
         scratch_shapes=[
             pltpu.VMEM((ZH, Y * rows, ZL * width), jnp.bfloat16),
-            pltpu.SemaphoreType.DMA((ZH, ZL)),
+            pltpu.SemaphoreType.DMA((2, ZH, ZL)),
         ],
         compiler_params=pltpu.CompilerParams(vmem_limit_bytes=48 * 1024 * 1024),
         cost_estimate=pl.CostEstimate(
             flops=4 * pairs * Y * X * cols * ZL * width, bytes_accessed=8 * 1024 * 1024, transcendentals=0
         ),
-    )(c.reshape(1).astype(jnp.int32), amps, gathered)
+    )(c.reshape(1).astype(jnp.int32), amps, gathered, last)
     got = lax.ppermute(other, "c", [(0, 1), (1, 0)])
     summed = (mine + got).reshape(Y * X, pairs * lines, 128)
     sums = lax.all_to_all(summed, ("y", "x"), 0, 0, tiled=True)

time: 163 us -> 164 us (level)
  starting transfers between devices: 2.61 us -> 13.8 us
  blocking collectives: 96 us -> 86.2 us
  waiting for transfers between devices: 34.4 us -> 28.6 us
  local copies, waits for them, and re-layouts: 8.56 us -> 13.6 us
    all_to_all x1 -> x0, blocking collectives: 50.4 us -> none  [per_device(): swapped = lax.all_to_all(masked, ('y', 'x', 'c'), 0, 0, tiled=True)]
    all_gather x0 -> x1, blocking collectives: none -> 40.7 us  [per_device(): lax.all_gather(last, ('zh', 'zl'), axis=0, tiled=True)]
    all_to_all x0 -> x1, starting transfers between devices: none -> 11.4 us  [per_device(): swapped = lax.all_to_all(masked, ('y', 'x', 'c'), 0, 0, tiled=True)]
    all_gather x1, waiting for transfers between devices: 32.8 us -> 27.1 us  [per_device(): gathered = lax.all_gather(most, ('zh', 'zl'), axis=0, tiled=True)]
    reshape x1, local copies, waits for them, and re-layouts: 0.65 us -> 2.52 us  [per_device(): swapped.reshape(Y * X, CORE, pairs, ZL, width).transpose(1, 2, 0, 3, 4)]
  transfers between devices with their start and end apart: 2 -> 3, of which waited for: 2 -> 2; matrix products, arithmetic and copies ran while one was open for 5% -> 8% of each run, Pallas kernels for 0% -> 0%
where the time goes in v5:
time: 164 us; the launch traced here: 163 us
  blocking collectives  86.2 us (53%)
  waiting for transfers between devices  28.6 us (17%)
  starting transfers between devices  13.8 us (8%)
  local copies, waits for them, and re-layouts  13.6 us (8%)
  between operations  13.5 us (8%)
  Pallas kernels  6.49 us (4%)
    all_gather x1, blocking collectives, per_device(): lax.all_gather(last, ('zh', 'zl'), axis=0, tiled=True)  40.7 us
    all_gather x1, waiting for transfers between devices, per_device(): gathered = lax.all_gather(most, ('zh', 'zl'), axis=0, tiled=True)  27.1 us
    all_to_all x1, blocking collectives, per_device(): sums = lax.all_to_all(summed, ('y', 'x'), 0, 0, tiled=True)  25.7 us
    all_to_all x1, blocking collectives, per_device(): moved = lax.all_to_all(ready, 'y', 0, 0, tiled=True)  19.9 us
    all_to_all x1, starting transfers between devices, per_device(): swapped = lax.all_to_all(masked, ('y', 'x', 'c'), 0, 0, tiled=True)  11.4 us
    pallas_call x1, Pallas kernels, per_device(): pl.pallas_call(ladder, out_shape=[jax.ShapeDtypeStruct((out_rows, 128), j...  4.46 us
    reshape x1, local copies, waits for them, and re-layouts, per_device(): amps = amps.reshape(CORE, pairs * Y * X, ZL * width)  3.56 us
  transfers between devices with their start and end apart: 3, of which 2 were waited for; matrix products, arithmetic and copies ran while one was open for 8% of the time, Pallas kernels for 0%

profile of v5, /device:TPU:1, one launch (start us, length us, event | category | flops | bytes accessed | tf_op | source)
XLA Modules:
  0.0 163.4 jit_solution(3209869708320785688)
XLA Ops:
  6.5 0.0 copy-start
  6.5 0.0 all-gather.2.cloned.1.call-start
  6.5 0.6 pad_add_fusion.where_ref
  7.2 0.0 copy-start.2
  7.2 0.0 copy-start.3
  7.2 0.0 copy-start.1
  7.2 2.0 %shard_map.64 = bf16[8,64,512]{2,1,0:T(8,128)(2,1)} custom-call(s32[2]{0:T(128)} %pad_add_fusion.where_ref, s32[48]{0:T(128)} %slab_ref.1, s32[16,256]{1,0:T(8,128)} %pattern_ref.1, bf16[64,4096]{1,0:T(8,128)(2,1)} %bitcast.44), custom_call_target="tpu_custom_call" | custom-call | tf_op jit(solution)/shard_map/pallas_call | solution.py:79
  9.2 19.9 %all_to_all.15 = bf16[8,64,512]{2,1,0:T(8,128)(2,1)S(1)} all-to-all(bf16[8,64,512]{2,1,0:T(8,128)(2,1)} %shard_map.64), channel_id=1, replica_groups=mesh['zh'=2,'y'=8,'zl'=6,'x'=4,'c'=2] {'y'}, dimensions={0} | all-to-all | bytes 1048576 | tf_op jit(solution)/shard_map/all_to_all | solution.py:85
  29.1 0.8 slice.17
  29.9 0.0 all-gather.2.cloned.1.call-update
  30.0 0.0 copy-done
  30.0 0.1 constant_dynamic-slice_fusion
  30.1 0.0 copy-done.2
  30.1 0.0 copy-done.3
  30.1 0.3 fusion
  30.4 0.0 copy-done.1
  30.4 0.2 broadcast_multiply_fusion
  30.6 2.0 %copy.11 = bf16[64,24,512]{2,1,0:T(8,128)(2,1)} copy(bf16[64,24,512]{2,0,1:T(8,128)(2,1)S(1)} %bitcast.39) | data formatting | bytes 3145728 | tf_op jit(solution)/shard_map/optimization_barrier | solution.py:97
  32.6 11.4 %all-to-all-start.1 = ((bf16[64,24,512]{2,1,0:T(8,128)(2,1)}), bf16[64,24,512]{2,1,0:T(8,128)(2,1)S(1)}, u32[]{:S(2)}, u32[]{:S(2)}) async-start(bf16[64,24,512]{2,1,0:T(8,128)(2,1)} %copy.11), calls=%async_computation.1 | async-start | bytes 3145728 | tf_op jit(solution)/shard_map/all_to_all | solution.py:98
  44.0 40.7 %all_gather.7 = bf16[768,512]{1,0:T(8,128)(2,1)S(1)} all-gather(bf16[64,512]{1,0:T(8,128)(2,1)S(1)} %slice_bitcast_fusion), channel_id=1, replica_groups=mesh['zh'=2,'y'=8,'zl'=6,'x'=4,'c'=2] {'zh','zl'}, dimensions={0}, use_global_device_ids=true | all-gather | bytes 851968 | tf_op jit(solution)/shard_map/all_gather | solution.py:99
  84.7 0.0 all-to-all-done.1
  84.7 1.7 %copy.12 = bf16[64,24,512]{2,0,1:T(8,128)(2,1)} copy(bf16[64,24,512]{2,1,0:T(8,128)(2,1)S(1)} %all-to-all-done.1) | data formatting | bytes 3145728 | tf_op jit(solution)/shard_map/all_to_all | solution.py:98
  86.3 2.5 %reshape.97 = bf16[32,2,4,6,512]{4,1,0,3,2:T(2,128)(2,1)S(1)} reshape(bf16[64,24,512]{2,0,1:T(8,128)(2,1)} %copy.12) | data formatting | bytes 3145728 | tf_op jit(solution)/shard_map/reshape | solution.py:100
  88.9 2.3 %copy.13 = bf16[2,4,32,6,512]{4,3,2,1,0:T(8,128)(2,1)} copy(bf16[2,4,32,6,512]{4,0,2,3,1:T(2,128)(2,1)S(1)} %bitcast.40) | data formatting | bytes 3145728 | tf_op jit(solution)/shard_map/transpose | solution.py:100
  91.1 3.6 %reshape.98.a_ref = bf16[2,128,3072]{2,1,0:T(8,128)(2,1)S(1)} reshape(bf16[2,4,32,6,512]{4,3,2,1,0:T(8,128)(2,1)} %copy.13) | data formatting | bytes 3145728 | tf_op jit(solution)/shard_map/reshape | solution.py:101
  94.7 27.1 %all-gather.2.cloned.1.call-done = bf16[5376,512]{1,0:T(8,128)(2,1)} async-done(((bf16[448,512]{1,0:T(8,128)(2,1)}), bf16[5376,512]{1,0:T(8,128)(2,1)}) %all-gather.2.cloned.1.call-update) | async-done | bytes 5505040 | tf_op jit(solution)/shard_map/all_gather | solution.py:87
  121.8 4.5 %shard_map.65 = (f32[1024,128]{1,0:T(8,128)S(1)}, f32[1024,128]{1,0:T(8,128)S(1)}) custom-call(s32[1]{0:T(128)} %bitcast.core_ref, bf16[2,128,3072]{2,1,0:T(8,128)(2,1)S(1)} %reshape.98.a_ref, bf16[2,6,448,512]{3,2,1,0:T(8,128)(2,1)} %bitcast.41, bf16[2,6,64,512]{3,2,1,0:T(8,128)(2,1)S(1)} %bitcast.38), custom_call_target="tpu_custom_call" | custom-call | flops 1610612736 | bytes 8388608 | tf_op jit(solution)/shard_map/pallas_call | solution.py:107
  126.3 2.4 %collective-permute-start = (f32[1024,128]{1,0:T(8,128)S(1)}, f32[1024,128]{1,0:T(8,128)S(1)}, u32[]{:S(2)}, u32[]{:S(2)}) collective-permute-start(f32[1024,128]{1,0:T(8,128)S(1)} %get-tuple-element.12), channel_id=1, source_target_pairs={{0,1},{1,0},{2,3},{3,2},{4,5},{5,4},{6,7},{7,6},{8,9},{9,8},{10,11... | collective-permute-start | bytes 1572872 | tf_op jit(solution)/shard_map/ppermute | solution.py:126
  128.7 1.5 collective-permute-done
  130.2 0.1 add.41
  130.2 25.7 %all_to_all.16 = f32[32,32,128]{2,1,0:T(8,128)S(1)} all-to-all(f32[32,32,128]{2,1,0:T(8,128)S(1)} %bitcast.42), channel_id=1, replica_groups=mesh['zh'=2,'y'=8,'zl'=6,'x'=4,'c'=2] {'y','x'}, dimensions={0} | all-to-all | bytes 1048576 | tf_op jit(solution)/shard_map/all_to_all | solution.py:128
  155.9 0.6 reshape.103
  (3 shorter events, 0.1 us)
Async XLA Ops:
  6.5 23.4 %copy-start = (s32[2,3072]{1,0:T(2,128)S(1)}, s32[2,3072]{1,0:T(2,128)}, u32[]{:S(2)}) copy-start(s32[2,3072]{1,0:T(2,128)} %param.11) | copy-start | bytes 73732
  6.5 115.3 %all-gather.2.cloned.1.call-start = ((), (), s32[]{:S(2)}) async-start(), calls=%async_computation.3 | async-start | bytes 5963776 | tf_op jit(solution)/shard_map/all_gather | solution.py:87
  7.2 22.9 %copy-start.2 = (s32[48]{0:T(128)S(1)}, s32[48]{0:T(128)}, u32[]{:S(2)}) copy-start(s32[48]{0:T(128)} %slab_ref.1) | copy-start | bytes 580
  7.2 22.9 %copy-start.3 = (s32[16,256]{1,0:T(8,128)S(1)}, s32[16,256]{1,0:T(8,128)}, u32[]{:S(2)}) copy-start(s32[16,256]{1,0:T(8,128)} %param.8) | copy-start | bytes 49156
  7.2 23.2 %copy-start.1 = (bf16[4,48,4096]{2,1,0:T(8,128)(2,1)S(1)}, bf16[4,48,4096]{2,1,0:T(8,128)(2,1)}, u32[]{:S(2)}) copy-start(bf16[4,48,4096]{2,1,0:T(8,128)(2,1)} %param.6) | copy-start | bytes 4718596
  32.6 52.1 %all-to-all-start.1 = ((bf16[64,24,512]{2,1,0:T(8,128)(2,1)}), bf16[64,24,512]{2,1,0:T(8,128)(2,1)S(1)}, u32[]{:S(2)}, u32[]{:S(2)}) async-start(bf16[64,24,512]{2,1,0:T(8,128)(2,1)} %copy.11), calls=%async_computation.1 | async-start | bytes 3145728 | tf_op jit(solution)/shard_map/all_to_all | solution.py:98
  126.3 3.9 %collective-permute-start = (f32[1024,128]{1,0:T(8,128)S(1)}, f32[1024,128]{1,0:T(8,128)S(1)}, u32[]{:S(2)}, u32[]{:S(2)}) collective-permute-start(f32[1024,128]{1,0:T(8,128)S(1)} %get-tuple-element.12), channel_id=1, source_target_pairs={{0,1},{1,0},{2,3},{3,2},{4,5},{5,4},{6,7},{7,6},{8,9},{9,8},{10,11... | collective-permute-start | bytes 1572872 | tf_op jit(solution)/shard_map/ppermute | solution.py:126
Sparse Core Ops, SparseCore 0:
  30.1 91.6 all-gather.1

commit v6 on v3

--- a/solution.py
+++ b/solution.py
@@ -19,16 +19,17 @@
     return (index_list[:, None] == jnp.arange(width, dtype=jnp.int32)[None, :]).astype(jnp.bfloat16)
 
 
-def split_depth(where_ref, slab_ref, pattern_ref, b_ref, out):
-    slab = slab_ref[where_ref[1]]
-    keep = pattern_ref[where_ref[0], slab].astype(jnp.float32).astype(jnp.bfloat16)
+def split_depth(slab_ref, pattern_ref, b_ref, out):
+    zh, y, zl, x, c = (lax.axis_index(name) for name in ALL)
+    slab = slab_ref[(zl * X + x) * CORE + c]
+    keep = pattern_ref[zh * Y + y, slab].astype(jnp.float32).astype(jnp.bfloat16)
     width = out.shape[2]
-    for y in range(Y):
-        out[y] = b_ref[:, y * width : (y + 1) * width] * keep
+    for k in range(Y):
+        out[k] = b_ref[:, k * width : (k + 1) * width] * keep
 
 
-def ladder(core_ref, a_ref, b_ref, mine_ref, other_ref, held, landed):
-    core = core_ref[0]
+def ladder(a_ref, b_ref, mine_ref, other_ref, held, landed):
+    core = lax.axis_index("c")
     width = b_ref.shape[3]
     copies = [
         [
@@ -45,8 +46,8 @@
     per = a_ref.shape[1]
     chips = Y * X
     stride = mine_ref.shape[0] // chips
-    columns = stride * chips // per
-    both = jnp.concatenate([a_ref[core], a_ref[1 - core]], axis=0)
+    fold = per // chips
+    both = a_ref[...].reshape(CORE * per, a_ref.shape[2])
     for zh, group in enumerate(copies):
         for copy in group:
             copy.wait()
@@ -54,13 +55,18 @@
             both, held[zh], (((1,), (1,)), ((), ())), preferred_element_type=jnp.float32
         )
         tiles = acc.shape[1] // 128
-        for t, out in enumerate((mine_ref, other_ref)):
-            for i in range(per // chips):
-                for k in range(tiles):
-                    start = t * per + i * chips
-                    out[pl.ds(i * columns + zh * tiles + k, chips, stride=stride), :] = acc[
-                        start : start + chips, k * 128 : (k + 1) * 128
-                    ]
+
+        def store(outs):
+            for t, out in enumerate(outs):
+                for i in range(fold):
+                    for k in range(tiles):
+                        start = t * per + i * chips
+                        out[pl.ds((zh * tiles + k) * fold + i, chips, stride=stride), :] = acc[
+                            start : start + chips, k * 128 : (k + 1) * 128
+                        ]
+
+        pl.when(core == 0)(functools.partial(store, (mine_ref, other_ref)))
+        pl.when(core != 0)(functools.partial(store, (other_ref, mine_ref)))
 
 
 def per_device(amplitudes, integrals, amp_pattern, int_pattern, slab_ids, pair_window):
@@ -75,9 +81,9 @@
     ready = pl.pallas_call(
         split_depth,
         out_shape=jax.ShapeDtypeStruct((Y, rows, width), jnp.bfloat16),
-        in_specs=[smem, smem, smem, pl.BlockSpec(memory_space=pltpu.VMEM)],
+        in_specs=[smem, smem, pl.BlockSpec(memory_space=pltpu.VMEM)],
         out_specs=pl.BlockSpec(memory_space=pltpu.VMEM),
-    )(jnp.stack([block, owner]).astype(jnp.int32), slab_ids, int_pattern, integrals.reshape(rows, depth))
+    )(slab_ids, int_pattern, integrals.reshape(rows, depth))
     moved = lax.all_to_all(ready, "y", 0, 0, tiled=True)
     gathered = lax.all_gather(moved.reshape(Y * rows, width), ("zh", "zl"), axis=0, tiled=True)
     gathered = gathered.reshape(ZH, ZL, Y * rows, width)
@@ -101,7 +107,7 @@
     mine, other = pl.pallas_call(
         ladder,
         out_shape=[jax.ShapeDtypeStruct((out_rows, 128), jnp.float32)] * 2,
-        in_specs=[smem, pl.BlockSpec(memory_space=pltpu.VMEM), pl.BlockSpec(memory_space=pltpu.HBM)],
+        in_specs=[pl.BlockSpec(memory_space=pltpu.VMEM), pl.BlockSpec(memory_space=pltpu.HBM)],
         out_specs=[pl.BlockSpec(memory_space=pltpu.VMEM)] * 2,
         scratch_shapes=[
             pltpu.VMEM((ZH, Y * rows, ZL * width), jnp.bfloat16),
@@ -111,11 +117,11 @@
         cost_estimate=pl.CostEstimate(
             flops=4 * pairs * Y * X * cols * ZL * width, bytes_accessed=8 * 1024 * 1024, transcendentals=0
         ),
-    )(c.reshape(1).astype(jnp.int32), amps, gathered)
+    )(amps, gathered)
     got = lax.ppermute(other, "c", [(0, 1), (1, 0)])
     summed = (mine + got).reshape(Y * X, pairs * lines, 128)
     sums = lax.all_to_all(summed, ("y", "x"), 0, 0, tiled=True)
-    return sums.sum(0).reshape(pairs, cols)
+    return sums.sum(0).reshape(lines, pairs, 128).transpose(1, 0, 2).reshape(pairs, cols)
 
 
 def solution(mesh):

time: 163 us -> 163 us (level)
  no operation moved by 1% of the time
where the time goes in v6:
time: 163 us; the launch traced here: 162 us
  blocking collectives  96 us (59%)
  waiting for transfers between devices  34.3 us (21%)
  between operations  13.5 us (8%)
  local copies, waits for them, and re-layouts  7.95 us (5%)
  Pallas kernels  6.96 us (4%)
  starting transfers between devices  2.48 us (2%)
    all_to_all x1, blocking collectives, per_device(): swapped = lax.all_to_all(masked, ('y', 'x', 'c'), 0, 0, tiled=True)  50.4 us
    all_gather x1, waiting for transfers between devices, per_device(): lax.all_gather(moved.reshape(Y * rows, width), ('zh', 'zl'), axis=0, tile...  32.8 us
    all_to_all x1, blocking collectives, per_device(): sums = lax.all_to_all(summed, ('y', 'x'), 0, 0, tiled=True)  25.6 us
    all_to_all x1, blocking collectives, per_device(): moved = lax.all_to_all(ready, 'y', 0, 0, tiled=True)  19.9 us
    pallas_call x1, Pallas kernels, per_device(): pl.pallas_call(ladder, out_shape=[jax.ShapeDtypeStruct((out_rows, 128), j...  4.93 us
    reshape x1, local copies, waits for them, and re-layouts, per_device(): amps = amps.reshape(CORE, pairs * Y * X, ZL * width)  3.56 us
  transfers between devices with their start and end apart: 2, of which 2 were waited for; matrix products, arithmetic and copies ran while one was open for 5% of the time, Pallas kernels for 0%

profile of v6, /device:TPU:1, one launch (start us, length us, event | category | flops | bytes accessed | tf_op | source)
XLA Modules:
  0.0 162.4 jit_solution(17981819460749472973)
XLA Ops:
  6.5 0.0 copy-start
  6.5 0.0 copy-start.2
  6.5 0.0 copy-start.3
  6.5 0.0 copy-start.1
  6.5 0.0 all-gather.2.cloned.1.call-start
  6.6 2.0 %shard_map.64 = bf16[8,64,512]{2,1,0:T(8,128)(2,1)} custom-call(s32[48]{0:T(128)} %slab_ref.1, s32[16,256]{1,0:T(8,128)} %pattern_ref.1, bf16[64,4096]{1,0:T(8,128)(2,1)} %bitcast.42), custom_call_target="tpu_custom_call" | custom-call | tf_op jit(solution)/shard_map/pallas_call | solution.py:81
  8.6 19.9 %all_to_all.15 = bf16[8,64,512]{2,1,0:T(8,128)(2,1)} all-to-all(bf16[8,64,512]{2,1,0:T(8,128)(2,1)} %shard_map.64), channel_id=1, replica_groups=mesh['zh'=2,'y'=8,'zl'=6,'x'=4,'c'=2] {'y'}, dimensions={0} | all-to-all | bytes 1048576 | tf_op jit(solution)/shard_map/all_to_all | solution.py:87
  28.5 0.0 all-gather.2.cloned.1.call-update
  28.6 0.0 copy-done
  28.6 0.1 constant_dynamic-slice_fusion
  28.7 0.0 copy-done.2
  28.7 0.0 copy-done.3
  28.7 0.3 fusion
  29.0 0.0 copy-done.1
  29.0 0.2 broadcast_multiply_fusion
  29.2 0.9 copy.11
  30.0 50.4 %all_to_all.16 = bf16[64,24,512]{2,1,0:T(8,128)(2,1)S(1)} all-to-all(bf16[64,24,512]{2,1,0:T(8,128)(2,1)S(1)} %copy.11), channel_id=1, replica_groups=mesh['zh'=2,'y'=8,'zl'=6,'x'=4,'c'=2] {'y','x','c'}, dimensions={0} | all-to-all | bytes 3145728 | tf_op jit(solution)/shard_map/all_to_all | solution.py:99
  80.5 0.5 copy.12
  81.0 0.6 reshape.93
  81.6 2.3 %copy.13 = bf16[2,4,32,6,512]{4,3,2,1,0:T(8,128)(2,1)} copy(bf16[2,4,32,6,512]{4,0,2,3,1:T(2,128)(2,1)S(1)} %bitcast.38) | data formatting | bytes 3145728 | tf_op jit(solution)/shard_map/transpose | solution.py:100
  83.9 3.6 %reshape.94.a_ref = bf16[2,128,3072]{2,1,0:T(8,128)(2,1)S(1)} reshape(bf16[2,4,32,6,512]{4,3,2,1,0:T(8,128)(2,1)} %copy.13) | data formatting | bytes 3145728 | tf_op jit(solution)/shard_map/reshape | solution.py:101
  87.5 32.8 %all-gather.2.cloned.1.call-done = bf16[6144,512]{1,0:T(8,128)(2,1)} async-done(((bf16[512,512]{1,0:T(8,128)(2,1)}), bf16[6144,512]{1,0:T(8,128)(2,1)}) %all-gather.2.cloned.1.call-update) | async-done | bytes 6291472 | tf_op jit(solution)/shard_map/all_gather | solution.py:88
  120.3 4.9 %shard_map.65 = (f32[1024,128]{1,0:T(8,128)S(1)}, f32[1024,128]{1,0:T(8,128)S(1)}) custom-call(bf16[2,128,3072]{2,1,0:T(8,128)(2,1)S(1)} %reshape.94.a_ref, bf16[2,6,512,512]{3,2,1,0:T(8,128)(2,1)} %bitcast.39), custom_call_target="tpu_custom_call" | custom-call | flops 1610612736 | bytes 8388608 | tf_op jit(solution)/shard_map/pallas_call | solution.py:107
  125.2 2.5 %collective-permute-start = (f32[1024,128]{1,0:T(8,128)S(1)}, f32[1024,128]{1,0:T(8,128)S(1)}, u32[]{:S(2)}, u32[]{:S(2)}) collective-permute-start(f32[1024,128]{1,0:T(8,128)S(1)} %get-tuple-element.10), channel_id=1, source_target_pairs={{0,1},{1,0},{2,3},{3,2},{4,5},{5,4},{6,7},{7,6},{8,9},{9,8},{10,11... | collective-permute-start | bytes 1572872 | tf_op jit(solution)/shard_map/ppermute | solution.py:121
  127.7 1.5 collective-permute-done
  129.2 0.1 add.41
  129.3 25.6 %all_to_all.17 = f32[32,32,128]{2,1,0:T(8,128)S(1)} all-to-all(f32[32,32,128]{2,1,0:T(8,128)S(1)} %bitcast.40), channel_id=1, replica_groups=mesh['zh'=2,'y'=8,'zl'=6,'x'=4,'c'=2] {'y','x'}, dimensions={0} | all-to-all | bytes 1048576 | tf_op jit(solution)/shard_map/all_to_all | solution.py:123
  154.9 0.6 reduce_sum.9
  (1 shorter events, 0.0 us)
Async XLA Ops:
  6.5 22.0 %copy-start = (s32[2,3072]{1,0:T(2,128)S(1)}, s32[2,3072]{1,0:T(2,128)}, u32[]{:S(2)}) copy-start(s32[2,3072]{1,0:T(2,128)} %param.11) | copy-start | bytes 73732
  6.5 22.1 %copy-start.2 = (s32[48]{0:T(128)S(1)}, s32[48]{0:T(128)}, u32[]{:S(2)}) copy-start(s32[48]{0:T(128)} %slab_ref.1) | copy-start | bytes 580
  6.5 22.1 %copy-start.3 = (s32[16,256]{1,0:T(8,128)S(1)}, s32[16,256]{1,0:T(8,128)}, u32[]{:S(2)}) copy-start(s32[16,256]{1,0:T(8,128)} %param.8) | copy-start | bytes 49156
  6.5 22.4 %copy-start.1 = (bf16[4,48,4096]{2,1,0:T(8,128)(2,1)S(1)}, bf16[4,48,4096]{2,1,0:T(8,128)(2,1)}, u32[]{:S(2)}) copy-start(bf16[4,48,4096]{2,1,0:T(8,128)(2,1)} %param.6) | copy-start | bytes 4718596
  6.5 113.7 %all-gather.2.cloned.1.call-start = ((), (), s32[]{:S(2)}) async-start(), calls=%async_computation.3 | async-start | bytes 6815744 | tf_op jit(solution)/shard_map/all_gather | solution.py:88
  125.2 4.0 %collective-permute-start = (f32[1024,128]{1,0:T(8,128)S(1)}, f32[1024,128]{1,0:T(8,128)S(1)}, u32[]{:S(2)}, u32[]{:S(2)}) collective-permute-start(f32[1024,128]{1,0:T(8,128)S(1)} %get-tuple-element.10), channel_id=1, source_target_pairs={{0,1},{1,0},{2,3},{3,2},{4,5},{5,4},{6,7},{7,6},{8,9},{9,8},{10,11... | collective-permute-start | bytes 1572872 | tf_op jit(solution)/shard_map/ppermute | solution.py:121
Sparse Core Ops, SparseCore 0:
  28.7 91.5 all-gather.1

commit v7 on v6

--- a/solution.py
+++ b/solution.py
@@ -1,5 +1,3 @@
-import functools
-
 import jax
 import jax.numpy as jnp
 from jax import lax
@@ -28,7 +26,7 @@
         out[k] = b_ref[:, k * width : (k + 1) * width] * keep
 
 
-def ladder(a_ref, b_ref, mine_ref, other_ref, held, landed):
+def ladder(a_ref, b_ref, mine_ref, other_ref, held, sums, landed):
     core = lax.axis_index("c")
     width = b_ref.shape[3]
     copies = [
@@ -51,22 +49,17 @@
     for zh, group in enumerate(copies):
         for copy in group:
             copy.wait()
-        acc = lax.dot_general(
+        sums[...] = lax.dot_general(
             both, held[zh], (((1,), (1,)), ((), ())), preferred_element_type=jnp.float32
         )
-        tiles = acc.shape[1] // 128
-
-        def store(outs):
-            for t, out in enumerate(outs):
-                for i in range(fold):
-                    for k in range(tiles):
-                        start = t * per + i * chips
-                        out[pl.ds((zh * tiles + k) * fold + i, chips, stride=stride), :] = acc[
-                            start : start + chips, k * 128 : (k + 1) * 128
-                        ]
-
-        pl.when(core == 0)(functools.partial(store, (mine_ref, other_ref)))
-        pl.when(core != 0)(functools.partial(store, (other_ref, mine_ref)))
+        tiles = sums.shape[1] // 128
+        for out, side in ((mine_ref, core), (other_ref, 1 - core)):
+            for i in range(fold):
+                picked = pl.ds(pl.multiple_of(side * per + i * chips, chips), chips)
+                for k in range(tiles):
+                    out[pl.ds((zh * tiles + k) * fold + i, chips, stride=stride), :] = sums[
+                        picked, k * 128 : (k + 1) * 128
+                    ]
 
 
 def per_device(amplitudes, integrals, amp_pattern, int_pattern, slab_ids, pair_window):
@@ -111,6 +104,7 @@
         out_specs=[pl.BlockSpec(memory_space=pltpu.VMEM)] * 2,
         scratch_shapes=[
             pltpu.VMEM((ZH, Y * rows, ZL * width), jnp.bfloat16),
+            pltpu.VMEM((CORE * pairs * Y * X, Y * rows), jnp.float32),
             pltpu.SemaphoreType.DMA((ZH, ZL)),
         ],
         compiler_params=pltpu.CompilerParams(vmem_limit_bytes=48 * 1024 * 1024),

time: 163 us -> 163 us (level)
  no operation moved by 1% of the time
where the time goes in v7:
time: 163 us; the launch traced here: 162 us
  blocking collectives  96 us (59%)
  waiting for transfers between devices  34.3 us (21%)
  between operations  13.5 us (8%)
  local copies, waits for them, and re-layouts  7.95 us (5%)
  Pallas kernels  6.88 us (4%)
  starting transfers between devices  2.62 us (2%)
    all_to_all x1, blocking collectives, per_device(): swapped = lax.all_to_all(masked, ('y', 'x', 'c'), 0, 0, tiled=True)  50.4 us
    all_gather x1, waiting for transfers between devices, per_device(): lax.all_gather(moved.reshape(Y * rows, width), ('zh', 'zl'), axis=0, tile...  32.8 us
    all_to_all x1, blocking collectives, per_device(): sums = lax.all_to_all(summed, ('y', 'x'), 0, 0, tiled=True)  25.6 us
    all_to_all x1, blocking collectives, per_device(): moved = lax.all_to_all(ready, 'y', 0, 0, tiled=True)  19.9 us
    pallas_call x1, Pallas kernels, per_device(): pl.pallas_call(ladder, out_shape=[jax.ShapeDtypeStruct((out_rows, 128), j...  4.84 us
    reshape x1, local copies, waits for them, and re-layouts, per_device(): amps = amps.reshape(CORE, pairs * Y * X, ZL * width)  3.56 us
  transfers between devices with their start and end apart: 2, of which 2 were waited for; matrix products, arithmetic and copies ran while one was open for 5% of the time, Pallas kernels for 0%

profile of v7, /device:TPU:1, one launch (start us, length us, event | category | flops | bytes accessed | tf_op | source)
XLA Modules:
  0.0 162.5 jit_solution(10360828541430982928)
XLA Ops:
  6.5 0.0 copy-start
  6.5 0.0 copy-start.2
  6.5 0.0 copy-start.3
  6.5 0.0 copy-start.1
  6.5 0.0 all-gather.2.cloned.1.call-start
  6.6 2.0 %shard_map.64 = bf16[8,64,512]{2,1,0:T(8,128)(2,1)} custom-call(s32[48]{0:T(128)} %slab_ref.1, s32[16,256]{1,0:T(8,128)} %pattern_ref.1, bf16[64,4096]{1,0:T(8,128)(2,1)} %bitcast.42), custom_call_target="tpu_custom_call" | custom-call | tf_op jit(solution)/shard_map/pallas_call | solution.py:74
  8.6 19.9 %all_to_all.15 = bf16[8,64,512]{2,1,0:T(8,128)(2,1)} all-to-all(bf16[8,64,512]{2,1,0:T(8,128)(2,1)} %shard_map.64), channel_id=1, replica_groups=mesh['zh'=2,'y'=8,'zl'=6,'x'=4,'c'=2] {'y'}, dimensions={0} | all-to-all | bytes 1048576 | tf_op jit(solution)/shard_map/all_to_all | solution.py:80
  28.5 0.0 all-gather.2.cloned.1.call-update
  28.6 0.0 copy-done
  28.6 0.1 constant_dynamic-slice_fusion
  28.7 0.0 copy-done.2
  28.7 0.0 copy-done.3
  28.7 0.3 fusion
  29.0 0.0 copy-done.1
  29.0 0.2 broadcast_multiply_fusion
  29.2 0.9 copy.11
  30.0 50.4 %all_to_all.16 = bf16[64,24,512]{2,1,0:T(8,128)(2,1)S(1)} all-to-all(bf16[64,24,512]{2,1,0:T(8,128)(2,1)S(1)} %copy.11), channel_id=1, replica_groups=mesh['zh'=2,'y'=8,'zl'=6,'x'=4,'c'=2] {'y','x','c'}, dimensions={0} | all-to-all | bytes 3145728 | tf_op jit(solution)/shard_map/all_to_all | solution.py:92
  80.5 0.5 copy.12
  81.0 0.6 reshape.93
  81.6 2.3 %copy.13 = bf16[2,4,32,6,512]{4,3,2,1,0:T(8,128)(2,1)} copy(bf16[2,4,32,6,512]{4,0,2,3,1:T(2,128)(2,1)S(1)} %bitcast.38) | data formatting | bytes 3145728 | tf_op jit(solution)/shard_map/transpose | solution.py:93
  83.9 3.6 %reshape.94.a_ref = bf16[2,128,3072]{2,1,0:T(8,128)(2,1)S(1)} reshape(bf16[2,4,32,6,512]{4,3,2,1,0:T(8,128)(2,1)} %copy.13) | data formatting | bytes 3145728 | tf_op jit(solution)/shard_map/reshape | solution.py:94
  87.5 32.8 %all-gather.2.cloned.1.call-done = bf16[6144,512]{1,0:T(8,128)(2,1)} async-done(((bf16[512,512]{1,0:T(8,128)(2,1)}), bf16[6144,512]{1,0:T(8,128)(2,1)}) %all-gather.2.cloned.1.call-update) | async-done | bytes 6291472 | tf_op jit(solution)/shard_map/all_gather | solution.py:81
  120.3 4.8 %shard_map.65 = (f32[1024,128]{1,0:T(8,128)S(1)}, f32[1024,128]{1,0:T(8,128)S(1)}) custom-call(bf16[2,128,3072]{2,1,0:T(8,128)(2,1)S(1)} %reshape.94.a_ref, bf16[2,6,512,512]{3,2,1,0:T(8,128)(2,1)} %bitcast.39), custom_call_target="tpu_custom_call" | custom-call | flops 1610612736 | bytes 8388608 | tf_op jit(solution)/shard_map/pallas_call | solution.py:100
  125.1 2.6 %collective-permute-start = (f32[1024,128]{1,0:T(8,128)S(1)}, f32[1024,128]{1,0:T(8,128)S(1)}, u32[]{:S(2)}, u32[]{:S(2)}) collective-permute-start(f32[1024,128]{1,0:T(8,128)S(1)} %get-tuple-element.10), channel_id=1, source_target_pairs={{0,1},{1,0},{2,3},{3,2},{4,5},{5,4},{6,7},{7,6},{8,9},{9,8},{10,11... | collective-permute-start | bytes 1572872 | tf_op jit(solution)/shard_map/ppermute | solution.py:115
  127.7 1.5 collective-permute-done
  129.2 0.1 add.41
  129.3 25.6 %all_to_all.17 = f32[32,32,128]{2,1,0:T(8,128)S(1)} all-to-all(f32[32,32,128]{2,1,0:T(8,128)S(1)} %bitcast.40), channel_id=1, replica_groups=mesh['zh'=2,'y'=8,'zl'=6,'x'=4,'c'=2] {'y','x'}, dimensions={0} | all-to-all | bytes 1048576 | tf_op jit(solution)/shard_map/all_to_all | solution.py:117
  155.0 0.6 reduce_sum.9
  (1 shorter events, 0.0 us)
Async XLA Ops:
  6.5 22.0 %copy-start = (s32[2,3072]{1,0:T(2,128)S(1)}, s32[2,3072]{1,0:T(2,128)}, u32[]{:S(2)}) copy-start(s32[2,3072]{1,0:T(2,128)} %param.11) | copy-start | bytes 73732
  6.5 22.1 %copy-start.2 = (s32[48]{0:T(128)S(1)}, s32[48]{0:T(128)}, u32[]{:S(2)}) copy-start(s32[48]{0:T(128)} %slab_ref.1) | copy-start | bytes 580
  6.5 22.1 %copy-start.3 = (s32[16,256]{1,0:T(8,128)S(1)}, s32[16,256]{1,0:T(8,128)}, u32[]{:S(2)}) copy-start(s32[16,256]{1,0:T(8,128)} %param.8) | copy-start | bytes 49156
  6.5 22.4 %copy-start.1 = (bf16[4,48,4096]{2,1,0:T(8,128)(2,1)S(1)}, bf16[4,48,4096]{2,1,0:T(8,128)(2,1)}, u32[]{:S(2)}) copy-start(bf16[4,48,4096]{2,1,0:T(8,128)(2,1)} %param.6) | copy-start | bytes 4718596
  6.5 113.7 %all-gather.2.cloned.1.call-start = ((), (), s32[]{:S(2)}) async-start(), calls=%async_computation.3 | async-start | bytes 6815744 | tf_op jit(solution)/shard_map/all_gather | solution.py:81
  125.1 4.1 %collective-permute-start = (f32[1024,128]{1,0:T(8,128)S(1)}, f32[1024,128]{1,0:T(8,128)S(1)}, u32[]{:S(2)}, u32[]{:S(2)}) collective-permute-start(f32[1024,128]{1,0:T(8,128)S(1)} %get-tuple-element.10), channel_id=1, source_target_pairs={{0,1},{1,0},{2,3},{3,2},{4,5},{5,4},{6,7},{7,6},{8,9},{9,8},{10,11... | collective-permute-start | bytes 1572872 | tf_op jit(solution)/shard_map/ppermute | solution.py:115
Sparse Core Ops, SparseCore 0:
  28.7 91.5 all-gather.1

commit v8 on v7

--- a/solution.py
+++ b/solution.py
@@ -26,8 +26,8 @@
         out[k] = b_ref[:, k * width : (k + 1) * width] * keep
 
 
-def ladder(a_ref, b_ref, mine_ref, other_ref, held, sums, landed):
-    core = lax.axis_index("c")
+def ladder(core_ref, a_ref, b_ref, mine_ref, other_ref, held, sums, landed):
+    core = core_ref[0]
     width = b_ref.shape[3]
     copies = [
         [
@@ -76,6 +76,7 @@
         out_shape=jax.ShapeDtypeStruct((Y, rows, width), jnp.bfloat16),
         in_specs=[smem, smem, pl.BlockSpec(memory_space=pltpu.VMEM)],
         out_specs=pl.BlockSpec(memory_space=pltpu.VMEM),
+        compiler_params=pltpu.CompilerParams(vmem_limit_bytes=8 * 1024 * 1024),
     )(slab_ids, int_pattern, integrals.reshape(rows, depth))
     moved = lax.all_to_all(ready, "y", 0, 0, tiled=True)
     gathered = lax.all_gather(moved.reshape(Y * rows, width), ("zh", "zl"), axis=0, tiled=True)
@@ -100,7 +101,7 @@
     mine, other = pl.pallas_call(
         ladder,
         out_shape=[jax.ShapeDtypeStruct((out_rows, 128), jnp.float32)] * 2,
-        in_specs=[pl.BlockSpec(memory_space=pltpu.VMEM), pl.BlockSpec(memory_space=pltpu.HBM)],
+        in_specs=[smem, pl.BlockSpec(memory_space=pltpu.VMEM), pl.BlockSpec(memory_space=pltpu.HBM)],
         out_specs=[pl.BlockSpec(memory_space=pltpu.VMEM)] * 2,
         scratch_shapes=[
             pltpu.VMEM((ZH, Y * rows, ZL * width), jnp.bfloat16),
@@ -111,7 +112,7 @@
         cost_estimate=pl.CostEstimate(
             flops=4 * pairs * Y * X * cols * ZL * width, bytes_accessed=8 * 1024 * 1024, transcendentals=0
         ),
-    )(amps, gathered)
+    )(c.reshape(1).astype(jnp.int32), amps, gathered)
     got = lax.ppermute(other, "c", [(0, 1), (1, 0)])
     summed = (mine + got).reshape(Y * X, pairs * lines, 128)
     sums = lax.all_to_all(summed, ("y", "x"), 0, 0, tiled=True)

time: 163 us -> 164 us (level)
  local copies, waits for them, and re-layouts: 7.95 us -> 10.4 us
    unnamed x8 -> x14, local copies, waits for them, and re-layouts: 0.02 us -> 2.45 us
where the time goes in v8:
time: 164 us
  blocking collectives  95.3 us (58%)
  waiting for transfers between devices  34.8 us (21%)
  between operations  13.5 us (8%)
  local copies, waits for them, and re-layouts  10.4 us (6%)
  Pallas kernels  5.83 us (4%)
  starting transfers between devices  2.58 us (2%)
    all_to_all x1, blocking collectives, per_device(): swapped = lax.all_to_all(masked, ('y', 'x', 'c'), 0, 0, tiled=True)  49.9 us
    all_gather x1, waiting for transfers between devices, per_device(): lax.all_gather(moved.reshape(Y * rows, width), ('zh', 'zl'), axis=0, tile...  33.3 us
    all_to_all x1, blocking collectives, per_device(): sums = lax.all_to_all(summed, ('y', 'x'), 0, 0, tiled=True)  25.6 us
    all_to_all x1, blocking collectives, per_device(): moved = lax.all_to_all(ready, 'y', 0, 0, tiled=True)  19.8 us
    pallas_call x1, Pallas kernels, per_device(): pl.pallas_call(ladder, out_shape=[jax.ShapeDtypeStruct((out_rows, 128), j...  4.96 us
    reshape x1, local copies, waits for them, and re-layouts, per_device(): amps = amps.reshape(CORE, pairs * Y * X, ZL * width)  3.58 us
  transfers between devices with their start and end apart: 2, of which 2 were waited for; matrix products, arithmetic and copies ran while one was open for 5% of the time, Pallas kernels for 0%

profile of v8, /device:TPU:1, one launch (start us, length us, event | category | flops | bytes accessed | tf_op | source)
XLA Modules:
  0.0 163.6 jit_solution(5037047329952668070)
XLA Ops:
  6.5 0.0 copy-start
  6.5 0.0 copy-start.4
  6.5 0.0 all-gather.2.cloned.1.call-start
  6.5 0.0 copy-start.1
  6.5 1.1 copy-done.1
  7.6 0.0 copy-start.2
  7.6 0.7 copy-done.2
  8.3 0.0 copy-start.3
  8.3 0.7 copy-done.3
  9.0 0.9 shard_map.64
  9.9 19.8 %all_to_all.15 = bf16[8,64,512]{2,1,0:T(8,128)(2,1)} all-to-all(bf16[8,64,512]{2,1,0:T(8,128)(2,1)S(1)} %shard_map.64), channel_id=1, replica_groups=mesh['zh'=2,'y'=8,'zl'=6,'x'=4,'c'=2] {'y'}, dimensions={0} | all-to-all | bytes 1048576 | tf_op jit(solution)/shard_map/all_to_all | solution.py:81
  29.7 0.0 all-gather.2.cloned.1.call-update
  29.7 0.0 copy-done
  29.7 0.1 constant_dynamic-slice_fusion
  29.8 0.0 copy-done.4
  29.8 0.0 copy-done.6
  29.8 0.3 fusion
  30.1 0.0 copy-done.5
  30.1 0.2 broadcast_multiply_fusion
  30.3 0.9 copy.11
  31.2 49.9 %all_to_all.16 = bf16[64,24,512]{2,1,0:T(8,128)(2,1)S(1)} all-to-all(bf16[64,24,512]{2,1,0:T(8,128)(2,1)S(1)} %copy.11), channel_id=1, replica_groups=mesh['zh'=2,'y'=8,'zl'=6,'x'=4,'c'=2] {'y','x','c'}, dimensions={0} | all-to-all | bytes 3145728 | tf_op jit(solution)/shard_map/all_to_all | solution.py:93
  81.1 0.5 copy.12
  81.5 0.6 reshape.97
  82.2 2.3 %copy.13 = bf16[2,4,32,6,512]{4,3,2,1,0:T(8,128)(2,1)} copy(bf16[2,4,32,6,512]{4,0,2,3,1:T(2,128)(2,1)S(1)} %bitcast.40) | data formatting | bytes 3145728 | tf_op jit(solution)/shard_map/transpose | solution.py:94
  84.5 3.6 %reshape.98.a_ref = bf16[2,128,3072]{2,1,0:T(8,128)(2,1)S(1)} reshape(bf16[2,4,32,6,512]{4,3,2,1,0:T(8,128)(2,1)} %copy.13) | data formatting | bytes 3145728 | tf_op jit(solution)/shard_map/reshape | solution.py:95
  88.1 33.3 %all-gather.2.cloned.1.call-done = bf16[6144,512]{1,0:T(8,128)(2,1)} async-done(((bf16[512,512]{1,0:T(8,128)(2,1)}), bf16[6144,512]{1,0:T(8,128)(2,1)}) %all-gather.2.cloned.1.call-update) | async-done | bytes 6291472 | tf_op jit(solution)/shard_map/all_gather | solution.py:82
  121.3 5.0 %shard_map.65 = (f32[1024,128]{1,0:T(8,128)S(1)}, f32[1024,128]{1,0:T(8,128)S(1)}) custom-call(s32[1]{0:T(128)} %bitcast.core_ref, bf16[2,128,3072]{2,1,0:T(8,128)(2,1)S(1)} %reshape.98.a_ref, bf16[2,6,512,512]{3,2,1,0:T(8,128)(2,1)} %bitcast.41), custom_call_target="tpu_custom_call" | custom-call | flops 1610612736 | bytes 8388608 | tf_op jit(solution)/shard_map/pallas_call | solution.py:101
  126.3 2.6 %collective-permute-start = (f32[1024,128]{1,0:T(8,128)S(1)}, f32[1024,128]{1,0:T(8,128)S(1)}, u32[]{:S(2)}, u32[]{:S(2)}) collective-permute-start(f32[1024,128]{1,0:T(8,128)S(1)} %get-tuple-element.10), channel_id=1, source_target_pairs={{0,1},{1,0},{2,3},{3,2},{4,5},{5,4},{6,7},{7,6},{8,9},{9,8},{10,11... | collective-permute-start | bytes 1572872 | tf_op jit(solution)/shard_map/ppermute | solution.py:116
  128.9 1.5 collective-permute-done
  130.4 0.1 add.41
  130.5 25.6 %all_to_all.17 = f32[32,32,128]{2,1,0:T(8,128)S(1)} all-to-all(f32[32,32,128]{2,1,0:T(8,128)S(1)} %bitcast.42), channel_id=1, replica_groups=mesh['zh'=2,'y'=8,'zl'=6,'x'=4,'c'=2] {'y','x'}, dimensions={0} | all-to-all | bytes 1048576 | tf_op jit(solution)/shard_map/all_to_all | solution.py:118
  156.1 0.6 reduce_sum.9
  (3 shorter events, 0.0 us)
Async XLA Ops:
  6.5 23.2 %copy-start = (s32[2,3072]{1,0:T(2,128)S(1)}, s32[2,3072]{1,0:T(2,128)}, u32[]{:S(2)}) copy-start(s32[2,3072]{1,0:T(2,128)} %param.11) | copy-start | bytes 73732
  6.5 23.3 %copy-start.4 = (s32[48]{0:T(128)S(1)}, s32[48]{0:T(128)}, u32[]{:S(2)}) copy-start(s32[48]{0:T(128)} %slab_ref.1) | copy-start | bytes 580
  6.5 114.8 %all-gather.2.cloned.1.call-start = ((), (), s32[]{:S(2)}) async-start(), calls=%async_computation.3 | async-start | bytes 6815744 | tf_op jit(solution)/shard_map/all_gather | solution.py:82
  6.5 1.1 copy-start.1
  7.6 0.7 copy-start.2
  8.3 0.7 copy-start.3
  9.0 20.9 %copy-start.6 = (s32[16,256]{1,0:T(8,128)S(1)}, s32[16,256]{1,0:T(8,128)}, u32[]{:S(2)}) copy-start(s32[16,256]{1,0:T(8,128)} %param.8) | copy-start | bytes 49156
  9.0 21.2 %copy-start.5 = (bf16[4,48,4096]{2,1,0:T(8,128)(2,1)S(1)}, bf16[4,48,4096]{2,1,0:T(8,128)(2,1)}, u32[]{:S(2)}) copy-start(bf16[4,48,4096]{2,1,0:T(8,128)(2,1)} %param.6) | copy-start | bytes 4718596
  126.3 4.1 %collective-permute-start = (f32[1024,128]{1,0:T(8,128)S(1)}, f32[1024,128]{1,0:T(8,128)S(1)}, u32[]{:S(2)}, u32[]{:S(2)}) collective-permute-start(f32[1024,128]{1,0:T(8,128)S(1)} %get-tuple-element.10), channel_id=1, source_target_pairs={{0,1},{1,0},{2,3},{3,2},{4,5},{5,4},{6,7},{7,6},{8,9},{9,8},{10,11... | collective-permute-start | bytes 1572872 | tf_op jit(solution)/shard_map/ppermute | solution.py:116
Sparse Core Ops, SparseCore 0:
  29.8 91.4 all-gather.1
